TPU v7x, 256 devices: a whole 4x4x8 slice. The times are simulated.
256 devices in a mesh: dp: 64 (over y, z, core), tensor: 4 (over x).
Axes of the slice: x: 4, y: 4, z: 8, core: 2. Of those that a mesh axis runs over, the one named last changes fastest.
Arguments:
- query_raw: bfloat16 [24576, 3072], P('dp', 'tensor'), may hold values from -8000 to 8000
- key_raw: bfloat16 [24576, 3072], P('dp', 'tensor'), may hold values from -8000 to 8000
- value_rows: bfloat16 [24576, 3072], P('dp', 'tensor'), may hold values from -24 to 24
- gain_query: float32 [3072], P('tensor'), may hold values from 0.1 to 1.9
- gain_key: float32 [3072], P('tensor'), may hold values from 0.1 to 1.9
- owner_id: int32 [24576], P('dp'), may hold values from 0 to 63, as said below
- utterance: int32 [24576], P('dp'), may hold values from 0 to 1, as said below
- cotangent: bfloat16 [49152, 3072], P('dp', 'tensor'), may hold values from -18 to 18
Outputs:
- attended: bfloat16 [49152, 3072], P('dp', 'tensor')
- grad_query: bfloat16 [24576, 3072], P('dp', 'tensor')
- grad_key: bfloat16 [24576, 3072], P('dp', 'tensor')
- grad_value: bfloat16 [24576, 3072], P('dp', 'tensor')
- gain_grad_query: float32 [3072], P('tensor')
- gain_grad_key: float32 [3072], P('tensor')
Inputs may be any that keep to these rules, and one draw needn't show every extreme that they name: `owner_id`: rows 2j and 2j+1 always have the same owner and the same utterance number. Of the 384 rows of one device at most 12 have the same owner; in every draw some owner gets 12 rows from every device. Rows with the same owner and the same number form one utterance.
All inputs are finite; a program needn't handle non-finite values.
Results may differ from a plain program's by a relative error of at most 0.017.
The roundings to bfloat16 on the way count: a program that leaves them out, or rounds other values in their place, can miss the bound.
Values may be sent and summed in bfloat16 or wider, within the bound.
A program may use at most 128 MiB of HBM per device.

v0:
```python
import functools
import math

import jax
import jax.numpy as jnp
from jax import lax
from jax.experimental import pallas as pl
from jax.experimental.pallas import tpu as pltpu
from jax.sharding import PartitionSpec as P

HD = 128
EPSILON = 1e-06
SLOT = 12
TILE = 16
HEADS = 6
GROUPS = 3
FAR = -(2.0**30)
F32 = jnp.float32
BF16 = jnp.bfloat16
MESH = pl.DeviceIdType.MESH
SHAPES = {64: (4, 8, 2), 16: (2, 4, 2), 8: (2, 2, 2)}


def mm(a, b):
    return lax.dot_general(a, b, (((1,), (0,)), ((), ())), preferred_element_type=F32)


def mm_nt(a, b):
    return lax.dot_general(a, b, (((1,), (1,)), ((), ())), preferred_element_type=F32)


def mm_tn(a, b):
    return lax.dot_general(a, b, (((0,), (0,)), ((), ())), preferred_element_type=F32)


def iota(shape, axis):
    return lax.broadcasted_iota(jnp.int32, shape, axis)


def ones_where(mask):
    return jnp.where(mask, 1.0, 0.0).astype(BF16)


def to_i32(x):
    return x.astype(jnp.int32)


def kernel(
    dp,
    tensors,
    tokens,
    query_ref,
    key_ref,
    value_ref,
    gain_query_ref,
    gain_key_ref,
    owner_ref,
    utterance_ref,
    cotangent_ref,
    attended_ref,
    grad_query_ref,
    grad_key_ref,
    grad_value_ref,
    gain_out_ref,
    pack_first,
    pack_second,
    pack_label,
    unpack_first,
    unpack_low,
    unpack_high_a,
    unpack_high_b,
    normed,
    inverse_query_ref,
    inverse_key_ref,
    send_value,
    recv_value,
    send_qk,
    recv_qk,
    back_qk,
    home_qk,
    back_value,
    home_value,
    value_own,
    grad_value_own,
    extend_query,
    extend_key,
    query_own,
    key_own,
    grad_query_own,
    key_sum,
    value_sum,
    grad_qn,
    grad_kn,
    stat_norm,
    stat_center,
    gain_near,
    gain_far,
    send_sems,
    recv_sems,
):
    size_y, size_z, size_c = SHAPES[dp]
    me = lax.axis_index("dp")
    my_x = lax.axis_index("tensor")
    my_c = me % size_c
    my_z = (me // size_c) % size_z
    my_y = me // (size_c * size_z)
    rows = dp * TILE
    own = dp * SLOT
    feat = HEADS * HD
    feat_total = feat * tensors
    blocks = dp // 16

    def peer_of(step):
        fast = step % size_z
        rest = step // size_z
        step_z = (fast % 2) * ((fast + 1) // 2) + (1 - fast % 2) * (size_z - fast // 2)
        to_y = (my_y + rest % size_y) % size_y
        to_z = (my_z + step_z) % size_z
        to_c = (my_c + rest // size_y) % size_c
        return (to_y * size_z + to_z) * size_c + to_c

    def scatter(source, target, index):
        own_copy = pltpu.make_async_copy(source.at[me], target.at[me], recv_sems.at[index])
        own_copy.start()

        def step_body(step, carry):
            peer = peer_of(step)
            pltpu.make_async_remote_copy(
                src_ref=source.at[peer],
                dst_ref=target.at[me],
                send_sem=send_sems.at[index],
                recv_sem=recv_sems.at[index],
                device_id={"dp": peer},
                device_id_type=MESH,
            ).start()
            return carry

        lax.fori_loop(1, dp, step_body, 0)

    def wait_recv(target, index):
        pltpu.make_async_copy(target, target, recv_sems.at[index]).wait()

    def wait_send(source, index, count):
        part = source.at[pl.ds(0, count)]
        pltpu.make_async_copy(part, part, send_sems.at[index]).wait()

    def share(buffer, slot, count, device_of, index):
        def step_body(step, carry):
            to = lax.rem(slot + step, count)
            pltpu.make_async_remote_copy(
                src_ref=buffer.at[slot],
                dst_ref=buffer.at[slot],
                send_sem=send_sems.at[index],
                recv_sem=recv_sems.at[index],
                device_id=device_of(to),
                device_id_type=MESH,
            ).start()
            return carry

        lax.fori_loop(1, count, step_body, 0)

    def share_wait(buffer, count, index):
        part = buffer.at[pl.ds(0, count - 1)]
        pltpu.make_async_copy(part, part, recv_sems.at[index]).wait()

    VALUE, QK, BACK_QK, BACK_VALUE, NORM, CENTER, NEAR, FARTHER = 0, 1, 4, 7, 8, 9, 10, 11

    owner_row = owner_ref[...]
    chosen = jnp.where(iota((dp, tokens), 0) == owner_row, 1.0, 0.0)
    upper = ones_where(iota((tokens, tokens), 0) < iota((tokens, tokens), 1))
    rank_row = jnp.sum(mm(chosen.astype(BF16), upper) * chosen, axis=0, keepdims=True)
    code_row_f = owner_row.astype(F32) * TILE + rank_row
    diagonal = iota((tokens, tokens), 0) == iota((tokens, tokens), 1)

    def as_column(row):
        return jnp.sum(jnp.where(diagonal, row, 0.0), axis=1, keepdims=True)

    rank_row = to_i32(rank_row)
    code_row = to_i32(code_row_f)
    none = -1

    def pack_block(block, carry):
        at = block * 256
        span = pl.ds(at, 256)
        row = iota((256, tokens), 0) + at
        pack_first[span, 0:tokens] = ones_where(row == code_row)
        pack_first[span, tokens : 2 * tokens] = ones_where(
            row == jnp.where(rank_row < 4, code_row + 12, none)
        )
        high = jnp.where(rank_row >= 4, code_row - 4, none)
        pack_second[span, 0:tokens] = ones_where(row == high)
        pack_second[span, tokens : 2 * tokens] = ones_where(
            row == jnp.where(rank_row >= 4, code_row + 4, none)
        )
        pack_label[span, :] = ones_where(row == jnp.where(rank_row < 8, code_row + 8, none))
        return carry

    lax.fori_loop(0, blocks, pack_block, 0)

    utterance_col = as_column(utterance_ref[...].astype(F32))
    lane = iota((tokens, HD), 1)
    label_low = ones_where(lane == to_i32(utterance_col))
    label_high = ones_where(lane == to_i32(utterance_col) + 64)

    def pack_value(block, carry):
        span = pl.ds(pl.multiple_of(block * 256, 256), 256)
        out = pl.ds(block * 16, 16)
        first = pack_first[span, :]
        second = pack_second[span, :]
        v = [value_ref[:, h * HD : (h + 1) * HD] for h in range(HEADS)]
        stack = lambda *parts: jnp.concatenate(parts, axis=0)

        def put(lo, part):
            width = part.shape[1]
            send_value[out, :, lo : lo + width] = part.astype(BF16).reshape(16, TILE, width)

        put(0, mm(first, stack(v[0], v[1])))
        put(128, mm(first, stack(v[2], v[3])))
        put(256, mm(second, stack(v[1], v[3])))
        put(384, mm(first, stack(v[4], v[5])))
        put(512, mm(second, stack(v[5], label_high)) + mm(pack_label[span, :], label_low))
        return carry

    lax.fori_loop(0, blocks, pack_value, 0)
    scatter(send_value, recv_value, VALUE)

    query_f = query_ref[...].astype(F32)
    key_f = key_ref[...].astype(F32)
    half = iota((tokens, HD), 1) < 64
    stat_norm[my_x] = jnp.where(
        half,
        jnp.sum(query_f * query_f, axis=1, keepdims=True),
        jnp.sum(key_f * key_f, axis=1, keepdims=True),
    )
    share(stat_norm, my_x, tensors, lambda to: {"tensor": to}, NORM)

    code_col = to_i32(as_column(code_row_f))
    rank_col = code_col % TILE
    column = iota((tokens, rows), 1)
    unpack_first[...] = ones_where(column == code_col)
    unpack_low[...] = ones_where(column == jnp.where(rank_col < 4, code_col + 12, none))
    unpack_high_a[...] = ones_where(column == jnp.where(rank_col >= 4, code_col - 4, none))
    unpack_high_b[...] = ones_where(column == jnp.where(rank_col >= 4, code_col + 4, none))

    share_wait(stat_norm, tensors, NORM)
    total = stat_norm[0]
    for x in range(1, tensors):
        total = total + stat_norm[x]
    inverse = lax.rsqrt(total / feat_total + EPSILON)
    inverse_query_ref[...] = jnp.broadcast_to(inverse[:, 0:1], (tokens, HD))
    inverse_key_ref[...] = jnp.broadcast_to(inverse[:, 64:65], (tokens, HD))
    for h in range(HEADS):
        cols = slice(h * HD, (h + 1) * HD)
        normed[0:tokens, cols] = (
            gain_query_ref[:, cols] * (query_ref[:, cols].astype(F32) * inverse_query_ref[...])
        ).astype(BF16)
        normed[tokens : 2 * tokens, cols] = (
            gain_key_ref[:, cols] * (key_ref[:, cols].astype(F32) * inverse_key_ref[...])
        ).astype(BF16)

    def pack_qk(group, carry):
        lo = pl.multiple_of(group * 256, 256)
        stacked = normed[:, pl.ds(lo, 256)]
        keys = stacked[tokens : 2 * tokens]
        high = jnp.concatenate([keys[:, 0:HD], keys[:, HD : 2 * HD]], axis=0)

        def block_body(block, inner):
            span = pl.ds(pl.multiple_of(block * 256, 256), 256)
            out = pl.ds(block * 16, 16)
            send_qk[group, out, :, 0:256] = (
                mm(pack_first[span, :], stacked).astype(BF16).reshape(16, TILE, 256)
            )
            send_qk[group, out, :, 256:384] = (
                mm(pack_second[span, :], high).astype(BF16).reshape(16, TILE, HD)
            )
            return inner

        lax.fori_loop(0, blocks, block_body, 0)
        scatter(send_qk.at[group], recv_qk.at[group], QK + group)
        return carry

    lax.fori_loop(0, GROUPS, pack_qk, 0)

    def own_maps(own_axis, message_axis, shape):
        row = iota(shape, own_axis)
        message = iota(shape, message_axis)
        base = (row // SLOT) * TILE
        slot = row % SLOT
        first = ones_where(message == base + slot)
        low = ones_where((message == base + 12 + slot) & (slot < 4))
        high_a = ones_where((message == base + slot - 4) & (slot >= 4))
        high_b = ones_where((message == base + slot + 4) & (slot >= 4))
        labels = ones_where(message == base + 8 + slot - jnp.where(slot < 8, 0, 4))
        return first, low, high_a, high_b, labels

    first, low, high_a, high_b, label_map = own_maps(0, 1, (192, 256))
    second_a = jnp.concatenate([low, high_a], axis=1)
    second_b = jnp.concatenate([low, high_b], axis=1)
    first_t, low_t, high_a_t, high_b_t, _ = own_maps(1, 0, (256, 192))
    back_first = jnp.concatenate([first_t, low_t], axis=1)
    back_second = jnp.concatenate([high_a_t, high_b_t], axis=1)

    wait_recv(recv_value, VALUE)

    def unpack_value(block, carry):
        span = pl.ds(pl.multiple_of(block * 192, 64), 192)
        src = pl.ds(block * 16, 16)
        t = [recv_value[src, :, i * HD : (i + 1) * HD].reshape(256, HD) for i in range(5)]
        stack = lambda *parts: jnp.concatenate(parts, axis=0)
        value_own[0, span, :] = mm(first, t[0]).astype(BF16)
        value_own[1, span, :] = mm(second_a, stack(t[0], t[2])).astype(BF16)
        value_own[2, span, :] = mm(first, t[1]).astype(BF16)
        value_own[3, span, :] = mm(second_b, stack(t[1], t[2])).astype(BF16)
        value_own[4, span, :] = mm(first, t[3]).astype(BF16)
        value_own[5, span, :] = mm(second_a, stack(t[3], t[4])).astype(BF16)
        found = mm(label_map, t[4])
        early = iota((192, 1), 0) % SLOT < 8
        is_zero = jnp.where(early, found[:, 0:1], found[:, 64:65])
        is_one = jnp.where(early, found[:, 1:2], found[:, 65:66])
        spot = iota((192, HD), 1)
        member = jnp.where(
            spot == 0, is_zero, jnp.where(spot == 1, is_one, 1.0 - is_zero - is_one)
        )
        used = spot < 3
        extend_key[span, :] = jnp.where(used, member, 0.0).astype(BF16)
        extend_query[span, :] = jnp.where(used, FAR * (1.0 - member), 0.0).astype(BF16)
        return carry

    lax.fori_loop(0, blocks, unpack_value, 0)

    factor = HD**-0.5
    scale = factor * math.log2(math.e)
    chunk = 256 if own % 256 == 0 else own

    def attention_group(group, carry):
        wait_recv(recv_qk.at[group], QK + group)

        def unpack_body(block, inner):
            span = pl.ds(pl.multiple_of(block * 192, 64), 192)
            src = pl.ds(block * 16, 16)
            both = recv_qk[group, src, :, 0:256].reshape(256, 256)
            high = recv_qk[group, src, :, 256:384].reshape(256, HD)
            q = mm(first, both).astype(BF16)
            query_own[0, span, :] = q[:, 0:HD]
            query_own[1, span, :] = q[:, HD : 2 * HD]
            key_own[0, span, :] = mm(
                second_a, jnp.concatenate([both[:, 0:HD], high], axis=0)
            ).astype(BF16)
            key_own[1, span, :] = mm(
                second_b, jnp.concatenate([both[:, HD : 2 * HD], high], axis=0)
            ).astype(BF16)
            return inner

        lax.fori_loop(0, blocks, unpack_body, 0)

        def head_body(local, inner):
            head = group * 2 + local
            key_sum[local] = jnp.zeros((own, HD), F32)
            value_sum[...] = jnp.zeros((own, HD), F32)
            keys = key_own[local]
            values = value_own[head]
            keys_wide = jnp.concatenate([keys, extend_key[...]], axis=1)
            cols = pl.ds(pl.multiple_of(head * HD, HD), HD)

            def row_body(index, deepest):
                span = pl.ds(pl.multiple_of(index * chunk, chunk), chunk)
                q = query_own[local, span, :]
                cot = cotangent_ref[span, cols]
                scores = mm_nt(jnp.concatenate([q, extend_query[span, :]], axis=1), keys_wide)
                raised = jnp.exp2((scores - jnp.max(scores, axis=1, keepdims=True)) * scale)
                weights = (raised * (1.0 / jnp.sum(raised, axis=1, keepdims=True))).astype(BF16)
                attended = mm(weights, values).astype(BF16)
                attended_ref[span, cols] = attended
                delta = jnp.sum(
                    cot.astype(F32) * attended.astype(F32), axis=1, keepdims=True
                )
                grad_weights = mm_nt(cot, values)
                grad_scores = (weights.astype(F32) * (grad_weights - delta)).astype(BF16)
                grad_query_own[local, span, :] = (mm(grad_scores, keys) * factor).astype(BF16)
                value_sum[...] += mm_tn(weights, cot)
                key_sum[local] += mm_tn(grad_scores, q)
                return deepest

            lax.fori_loop(0, own // chunk, row_body, 0)
            grad_value_own[head] = value_sum[...].astype(BF16)
            return inner

        lax.fori_loop(0, 2, head_body, 0)

        def pack_body(block, inner):
            span = pl.ds(pl.multiple_of(block * 192, 64), 192)
            out = pl.ds(block * 16, 16)
            q_a = grad_query_own[0, span, :]
            q_b = grad_query_own[1, span, :]
            k_a = (key_sum[0, span, :] * factor).astype(BF16)
            k_b = (key_sum[1, span, :] * factor).astype(BF16)
            stacked = jnp.concatenate(
                [jnp.concatenate([q_a, q_b], axis=1), jnp.concatenate([k_a, k_b], axis=1)],
                axis=0,
            )
            back_qk[group, out, :, 0:256] = (
                mm(back_first, stacked).astype(BF16).reshape(16, TILE, 256)
            )
            back_qk[group, out, :, 256:384] = (
                mm(back_second, jnp.concatenate([k_a, k_b], axis=0))
                .astype(BF16)
                .reshape(16, TILE, HD)
            )
            return inner

        lax.fori_loop(0, blocks, pack_body, 0)
        scatter(back_qk.at[group], home_qk.at[group], BACK_QK + group)
        return carry

    lax.fori_loop(0, GROUPS, attention_group, 0)

    def pack_grad_value(block, carry):
        span = pl.ds(pl.multiple_of(block * 192, 64), 192)
        out = pl.ds(block * 16, 16)
        v = [grad_value_own[h, span, :] for h in range(HEADS)]
        stack = lambda *parts: jnp.concatenate(parts, axis=0)

        def put(lo, part):
            back_value[out, :, lo : lo + HD] = part.astype(BF16).reshape(16, TILE, HD)

        put(0, mm(back_first, stack(v[0], v[1])))
        put(128, mm(back_first, stack(v[2], v[3])))
        put(256, mm(back_second, stack(v[1], v[3])))
        put(384, mm(back_first, stack(v[4], v[5])))
        put(512, mm(high_a_t, v[5]))
        return carry

    lax.fori_loop(0, blocks, pack_grad_value, 0)
    scatter(back_value, home_value, BACK_VALUE)

    def unpack_home(group, carry):
        wait_recv(home_qk.at[group], BACK_QK + group)
        both = home_qk[group, :, :, 0:256].reshape(rows, 256)
        high = home_qk[group, :, :, 256:384].reshape(rows, HD)
        lo = pl.multiple_of(group * 256, 256)
        grad_qn[:, pl.ds(lo, 256)] = mm(unpack_first[...], both).astype(BF16)
        keys = mm(unpack_low[...], both)
        grad_kn[:, pl.ds(lo, HD)] = (keys[:, 0:HD] + mm(unpack_high_a[...], high)).astype(BF16)
        grad_kn[:, pl.ds(lo + HD, HD)] = (
            keys[:, HD : 2 * HD] + mm(unpack_high_b[...], high)
        ).astype(BF16)
        return carry

    lax.fori_loop(0, GROUPS, unpack_home, 0)

    near = my_y * size_c + my_c
    near_count = size_y * size_c
    center_q = jnp.zeros((tokens, HD), F32)
    center_k = jnp.zeros((tokens, HD), F32)
    gain_near[near] = jnp.zeros((8, feat), F32)
    for h in range(HEADS):
        cols = slice(h * HD, (h + 1) * HD)
        term = grad_qn[:, cols].astype(F32) * (
            query_ref[:, cols].astype(F32) * inverse_query_ref[...]
        )
        gain_near[near, 0:1, cols] = jnp.sum(term, axis=0, keepdims=True)
        center_q = center_q + gain_query_ref[:, cols] * term
        term = grad_kn[:, cols].astype(F32) * (
            key_ref[:, cols].astype(F32) * inverse_key_ref[...]
        )
        gain_near[near, 1:2, cols] = jnp.sum(term, axis=0, keepdims=True)
        center_k = center_k + gain_key_ref[:, cols] * term
    stat_center[my_x] = jnp.where(
        half,
        jnp.sum(center_q, axis=1, keepdims=True),
        jnp.sum(center_k, axis=1, keepdims=True),
    )
    share(stat_center, my_x, tensors, lambda to: {"tensor": to}, CENTER)
    share(
        gain_near,
        near,
        near_count,
        lambda to: {"dp": ((to // size_c) * size_z + my_z) * size_c + to % size_c},
        NEAR,
    )
    share_wait(stat_center, tensors, CENTER)
    total = stat_center[0]
    for x in range(1, tensors):
        total = total + stat_center[x]
    total = total / feat_total
    center_q = jnp.broadcast_to(total[:, 0:1], (tokens, HD))
    center_k = jnp.broadcast_to(total[:, 64:65], (tokens, HD))
    for h in range(HEADS):
        cols = slice(h * HD, (h + 1) * HD)
        inverse = inverse_query_ref[...]
        unit = query_ref[:, cols].astype(F32) * inverse
        scaled = gain_query_ref[:, cols] * grad_qn[:, cols].astype(F32)
        grad_query_ref[:, cols] = ((scaled - unit * center_q) * inverse).astype(BF16)
        inverse = inverse_key_ref[...]
        unit = key_ref[:, cols].astype(F32) * inverse
        scaled = gain_key_ref[:, cols] * grad_kn[:, cols].astype(F32)
        grad_key_ref[:, cols] = ((scaled - unit * center_k) * inverse).astype(BF16)

    share_wait(gain_near, near_count, NEAR)
    total = gain_near[0]
    for i in range(1, near_count):
        total = total + gain_near[i]
    gain_far[my_z] = total
    share(
        gain_far,
        my_z,
        size_z,
        lambda to: {"dp": (my_y * size_z + to) * size_c + my_c},
        FARTHER,
    )

    wait_recv(home_value, BACK_VALUE)
    t = [home_value[:, :, i * HD : (i + 1) * HD].reshape(rows, HD) for i in range(5)]
    unpacked = (
        mm(unpack_first[...], t[0]),
        mm(unpack_low[...], t[0]) + mm(unpack_high_a[...], t[2]),
        mm(unpack_first[...], t[1]),
        mm(unpack_low[...], t[1]) + mm(unpack_high_b[...], t[2]),
        mm(unpack_first[...], t[3]),
        mm(unpack_low[...], t[3]) + mm(unpack_high_a[...], t[4]),
    )
    for h in range(HEADS):
        grad_value_ref[:, h * HD : (h + 1) * HD] = unpacked[h].astype(BF16)

    share_wait(gain_far, size_z, FARTHER)
    total = gain_far[0]
    for i in range(1, size_z):
        total = total + gain_far[i]
    gain_out_ref[...] = total

    wait_send(send_value, VALUE, dp - 1)
    for group in range(GROUPS):
        wait_send(send_qk.at[group], QK + group, dp - 1)
        wait_send(back_qk.at[group], BACK_QK + group, dp - 1)
    wait_send(back_value, BACK_VALUE, dp - 1)
    wait_send(stat_norm, NORM, tensors - 1)
    wait_send(stat_center, CENTER, tensors - 1)
    wait_send(gain_near, NEAR, near_count - 1)
    wait_send(gain_far, FARTHER, size_z - 1)


def shards(query_raw, key_raw, value_rows, gain_query, gain_key, owner_id, utterance, cotangent):
    dp = lax.axis_size("dp")
    tensors = lax.axis_size("tensor")
    tokens, feat = query_raw.shape
    rows = dp * TILE
    own = dp * SLOT
    _, size_z, _ = SHAPES[dp]
    vmem = pl.BlockSpec(memory_space=pltpu.VMEM)
    out_shape = (
        jax.ShapeDtypeStruct((own, feat), BF16),
        jax.ShapeDtypeStruct((tokens, feat), BF16),
        jax.ShapeDtypeStruct((tokens, feat), BF16),
        jax.ShapeDtypeStruct((tokens, feat), BF16),
        jax.ShapeDtypeStruct((8, feat), F32),
    )
    scratch = [
        pltpu.VMEM((rows, 2 * tokens), BF16),
        pltpu.VMEM((rows, 2 * tokens), BF16),
        pltpu.VMEM((rows, tokens), BF16),
        pltpu.VMEM((tokens, rows), BF16),
        pltpu.VMEM((tokens, rows), BF16),
        pltpu.VMEM((tokens, rows), BF16),
        pltpu.VMEM((tokens, rows), BF16),
        pltpu.VMEM((2 * tokens, feat), BF16),
        pltpu.VMEM((tokens, HD), F32),
        pltpu.VMEM((tokens, HD), F32),
        pltpu.VMEM((dp, TILE, 640), BF16),
        pltpu.VMEM((dp, TILE, 640), BF16),
        pltpu.VMEM((GROUPS, dp, TILE, 384), BF16),
        pltpu.VMEM((GROUPS, dp, TILE, 384), BF16),
        pltpu.VMEM((GROUPS, dp, TILE, 384), BF16),
        pltpu.VMEM((GROUPS, dp, TILE, 384), BF16),
        pltpu.VMEM((dp, TILE, 640), BF16),
        pltpu.VMEM((dp, TILE, 640), BF16),
        pltpu.VMEM((HEADS, own, HD), BF16),
        pltpu.VMEM((HEADS, own, HD), BF16),
        pltpu.VMEM((own, HD), BF16),
        pltpu.VMEM((own, HD), BF16),
        pltpu.VMEM((2, own, HD), BF16),
        pltpu.VMEM((2, own, HD), BF16),
        pltpu.VMEM((2, own, HD), BF16),
        pltpu.VMEM((2, own, HD), F32),
        pltpu.VMEM((own, HD), F32),
        pltpu.VMEM((tokens, feat), BF16),
        pltpu.VMEM((tokens, feat), BF16),
        pltpu.VMEM((tensors, tokens, HD), F32),
        pltpu.VMEM((tensors, tokens, HD), F32),
        pltpu.VMEM((dp // size_z, 8, feat), F32),
        pltpu.VMEM((size_z, 8, feat), F32),
        pltpu.SemaphoreType.DMA((12,)),
        pltpu.SemaphoreType.DMA((12,)),
    ]
    attended, grad_query, grad_key, grad_value, gains = pl.pallas_call(
        functools.partial(kernel, dp, tensors, tokens),
        out_shape=out_shape,
        in_specs=[vmem] * 8,
        out_specs=[vmem] * 5,
        scratch_shapes=scratch,
        compiler_params=pltpu.CompilerParams(
            has_side_effects=True, vmem_limit_bytes=58 * 1024 * 1024
        ),
    )(
        query_raw,
        key_raw,
        value_rows,
        gain_query[None, :],
        gain_key[None, :],
        owner_id[None, :],
        utterance[None, :],
        cotangent,
    )
    return (attended, grad_query, grad_key, grad_value, gains[0], gains[1])


def solution(mesh):
    wide = P("dp", "tensor")
    return jax.shard_map(
        shards,
        mesh=mesh,
        in_specs=(wide, wide, wide, P("tensor"), P("tensor"), P("dp"), P("dp"), wide),
        out_specs=(wide, wide, wide, wide, P("tensor"), P("tensor")),
        check_vma=False,
    )
```

profile of v0, /device:TPU:1, one launch (start us, length us, event | category | flops | bytes accessed | tf_op | source)
XLA Modules:
  0.0 201.9 jit_solution(8447742574867484961)
XLA Ops:
  0.6 1.3 broadcast_in_dim.12.gain_query_ref
  1.9 1.3 broadcast_in_dim.13.gain_key_ref
  3.2 1.2 broadcast_in_dim.14.owner_ref
  4.4 1.2 broadcast_in_dim.15.utterance_ref
  5.7 189.9 %shard_map.127 = (bf16[768,768]{1,0:T(8,128)(2,1)}, bf16[384,768]{1,0:T(8,128)(2,1)}, bf16[384,768]{1,0:T(8,128)(2,1)}, bf16[384,768]{1,0:T(8,128)(2,1)}, f32[8,768]{1,0:T(8,128)}) custom-call(bf16[384,768]{1,0:T(8,128)(2,1)} %query_ref.1, bf16[384,768]{1,0:T(8,128)(2,1)} %key_ref.1, bf16[384,768]{1,0:T(8,128)(2,1)} %value_ref.1, ...), custom_call_target="tpu_custom_call" | custom-call | tf_op jit(solution)/shard_map/pallas_call | solution.py:594
  195.5 1.4 slice_reduce_fusion
  197.0 0.0 copy-start.2
  197.0 0.0 copy-start.1
  197.0 2.5 %copy.18 = bf16[768,768]{1,0:T(8,128)(2,1)} copy(bf16[768,768]{1,0:T(8,128)(2,1)} %get-tuple-element.24) | data formatting | bytes 2359296
  199.4 0.0 copy-done.2
  199.4 0.0 copy-start
  199.4 0.8 copy.19
  200.2 0.0 copy-done.1
  200.2 0.8 copy.20
  201.1 0.0 copy-done
  201.1 0.8 copy.21
Async XLA Ops:
  197.0 2.5 %copy-start.2 = (bf16[384,768]{1,0:T(8,128)(2,1)S(1)}, bf16[384,768]{1,0:T(8,128)(2,1)}, u32[]{:S(2)}) copy-start(bf16[384,768]{1,0:T(8,128)(2,1)} %get-tuple-element.25) | copy-start | bytes 1769476
  197.0 3.3 %copy-start.1 = (bf16[384,768]{1,0:T(8,128)(2,1)S(1)}, bf16[384,768]{1,0:T(8,128)(2,1)}, u32[]{:S(2)}) copy-start(bf16[384,768]{1,0:T(8,128)(2,1)} %get-tuple-element.26) | copy-start | bytes 1769476
  199.4 1.6 copy-start
where the time goes:
time: 202 us
  Pallas kernels  190 us (94%)
  local copies, waits for them, and re-layouts  11.4 us (6%)
    pallas_call x1, Pallas kernels, shards(): pl.pallas_call(functools.partial(kernel, dp, tensors, tokens), out_shape=...  190 us
    unnamed x10, local copies, waits for them, and re-layouts  4.91 us

commit v1 on v0

v1 whole, which is shorter than its diff:
```python
import functools
import math

import jax
import jax.numpy as jnp
from jax import lax
from jax.experimental import pallas as pl
from jax.experimental.pallas import tpu as pltpu
from jax.sharding import PartitionSpec as P

HD = 128
EPSILON = 1e-06
SLOT = 12
TILE = 16
HEADS = 6
GROUPS = 3
FAR = -(2.0**30)
F32 = jnp.float32
BF16 = jnp.bfloat16
MESH = pl.DeviceIdType.MESH
STRIDE = 23
SHAPES = {64: (4, 8, 2), 16: (2, 4, 2)}


def mm(a, b):
    return lax.dot_general(a, b, (((1,), (0,)), ((), ())), preferred_element_type=F32)


def mm_nt(a, b):
    return lax.dot_general(a, b, (((1,), (1,)), ((), ())), preferred_element_type=F32)


def iota(shape, axis):
    return lax.broadcasted_iota(jnp.int32, shape, axis)


def ones_where(mask):
    return jnp.where(mask, 1.0, 0.0).astype(BF16)


def to_i32(x):
    return x.astype(jnp.int32)


def over(*parts):
    return jnp.concatenate(parts, axis=0)


def beside(*parts):
    return jnp.concatenate(parts, axis=1)


def kernel(
    dp,
    tensors,
    tokens,
    query_ref,
    key_ref,
    value_ref,
    gain_query_ref,
    gain_key_ref,
    owner_ref,
    utterance_ref,
    cotangent_hbm,
    attended_hbm,
    grad_query_ref,
    grad_key_ref,
    grad_value_ref,
    gain_query_out,
    gain_key_out,
    pack_first,
    pack_second,
    unpack_first,
    unpack_low,
    unpack_high_a,
    unpack_high_b,
    normed,
    inverse_query_ref,
    inverse_key_ref,
    out_0,
    out_1,
    out_2,
    out_3,
    in_0,
    in_1,
    in_2,
    in_3,
    back_0,
    back_1,
    back_2,
    back_3,
    home_0,
    home_1,
    home_2,
    home_3,
    value_own,
    grad_value_own,
    extend_query,
    extend_key,
    query_own,
    key_own,
    grad_query_own,
    grad_key_own,
    key_sum,
    value_sum,
    grad_qn,
    grad_kn,
    center_query_ref,
    center_key_ref,
    stat_norm,
    stat_center,
    gain_near,
    gain_far,
    cotangent_ref,
    attended_ref,
    send_sems,
    recv_sems,
    local_sems,
):
    size_y, size_z, size_c = SHAPES[dp]
    me = lax.axis_index("dp")
    my_x = lax.axis_index("tensor")
    my_c = me % size_c
    my_z = (me // size_c) % size_z
    my_y = me // (size_c * size_z)
    rows = dp * TILE
    own = dp * SLOT
    feat = HEADS * HD
    feat_total = feat * tensors
    blocks = dp // 16

    def scatter(source, target, index):
        pltpu.make_async_copy(source.at[me], target.at[me], recv_sems.at[index]).start()

        def step_body(step, carry):
            peer = lax.rem(me + step * STRIDE, dp)
            pltpu.make_async_remote_copy(
                src_ref=source.at[peer],
                dst_ref=target.at[me],
                send_sem=send_sems.at[index],
                recv_sem=recv_sems.at[index],
                device_id={"dp": peer},
                device_id_type=MESH,
            ).start()
            return carry

        lax.fori_loop(1, dp, step_body, 0)

    def wait_recv(target, index):
        pltpu.make_async_copy(target, target, recv_sems.at[index]).wait()

    def wait_send(source, index, count):
        part = source.at[pl.ds(0, count)]
        pltpu.make_async_copy(part, part, send_sems.at[index]).wait()

    def share(buffer, slot, count, device_of, index):
        def step_body(step, carry):
            to = lax.rem(slot + step, count)
            pltpu.make_async_remote_copy(
                src_ref=buffer.at[slot],
                dst_ref=buffer.at[slot],
                send_sem=send_sems.at[index],
                recv_sem=recv_sems.at[index],
                device_id=device_of(to),
                device_id_type=MESH,
            ).start()
            return carry

        lax.fori_loop(1, count, step_body, 0)

    def share_wait(buffer, count, index):
        part = buffer.at[pl.ds(0, count - 1)]
        pltpu.make_async_copy(part, part, recv_sems.at[index]).wait()

    OUT, BACK, NORM, CENTER, NEAR, FARTHER = 0, 4, 8, 9, 10, 11

    load_cotangent = pltpu.make_async_copy(cotangent_hbm, cotangent_ref, local_sems.at[0])
    load_cotangent.start()

    half = iota((tokens, HD), 1) < 64
    query_f = query_ref[...].astype(F32)
    key_f = key_ref[...].astype(F32)
    stat_norm[my_x] = jnp.where(
        half,
        jnp.sum(query_f * query_f, axis=1, keepdims=True),
        jnp.sum(key_f * key_f, axis=1, keepdims=True),
    )
    share(stat_norm, my_x, tensors, lambda to: {"tensor": to}, NORM)

    owner_row = owner_ref[...].reshape(1, tokens)
    chosen = jnp.where(iota((dp, tokens), 0) == owner_row, 1.0, 0.0)
    upper = ones_where(iota((tokens, tokens), 0) < iota((tokens, tokens), 1))
    rank_row = jnp.sum(mm(chosen.astype(BF16), upper) * chosen, axis=0, keepdims=True)
    code_row_f = owner_row.astype(F32) * TILE + rank_row
    diagonal = iota((tokens, tokens), 0) == iota((tokens, tokens), 1)

    def as_column(row):
        return jnp.sum(jnp.where(diagonal, row, 0.0), axis=1, keepdims=True)

    rank_row = to_i32(rank_row)
    code_row = to_i32(code_row_f)
    none = -1

    utterance_col = to_i32(as_column(utterance_ref[...].reshape(1, tokens).astype(F32)))
    lane = iota((tokens, HD), 1)
    label_low = ones_where(lane == utterance_col)
    label_high = ones_where(lane == utterance_col + 64)

    def value_head(h):
        return value_ref[:, h * HD : (h + 1) * HD]

    def put(buffer, out, lo, part):
        width = part.shape[1]
        buffer[out, :, lo : lo + width] = part.astype(BF16).reshape(16, TILE, width)

    def pack_0(block, carry):
        span = pl.ds(pl.multiple_of(block * 256, 256), 256)
        out = pl.ds(block * 16, 16)
        row = iota((256, tokens), 0) + block * 256
        first = beside(
            ones_where(row == code_row),
            ones_where(row == jnp.where(rank_row < 4, code_row + 12, none)),
        )
        second = beside(
            ones_where(row == jnp.where(rank_row >= 4, code_row - 4, none)),
            ones_where(row == jnp.where(rank_row >= 4, code_row + 4, none)),
        )
        third = ones_where(row == jnp.where(rank_row < 8, code_row + 8, none))
        pack_first[span, :] = first
        pack_second[span, :] = second
        put(out_0, out, 0, mm(first, over(value_head(0), value_head(1))))
        put(out_0, out, HD, mm(second, over(value_head(1), label_high)) + mm(third, label_low))
        return carry

    lax.fori_loop(0, blocks, pack_0, 0)
    scatter(out_0, in_0, OUT)

    share_wait(stat_norm, tensors, NORM)
    total = stat_norm[0]
    for x in range(1, tensors):
        total = total + stat_norm[x]
    inverse = lax.rsqrt(total / feat_total + EPSILON)
    inverse_query_ref[...] = jnp.broadcast_to(inverse[:, 0:1], (tokens, HD))
    inverse_key_ref[...] = jnp.broadcast_to(inverse[:, 64:65], (tokens, HD))

    def gain_of(ref, h):
        return ref[h * HD : (h + 1) * HD].reshape(1, HD)

    def unit_query(h):
        return query_ref[:, h * HD : (h + 1) * HD].astype(F32) * inverse_query_ref[...]

    def unit_key(h):
        return key_ref[:, h * HD : (h + 1) * HD].astype(F32) * inverse_key_ref[...]

    def pack_qk(group, buffer, index):
        for h in (2 * group, 2 * group + 1):
            cols = slice(h * HD, (h + 1) * HD)
            normed[0:tokens, cols] = (gain_of(gain_query_ref, h) * unit_query(h)).astype(BF16)
            normed[tokens : 2 * tokens, cols] = (
                gain_of(gain_key_ref, h) * unit_key(h)
            ).astype(BF16)
        lo = group * 256

        def block_body(block, carry):
            span = pl.ds(pl.multiple_of(block * 256, 256), 256)
            out = pl.ds(block * 16, 16)
            first = pack_first[span, :]
            second = pack_second[span, :]
            keys = slice(tokens, 2 * tokens)
            put(buffer, out, 0, mm(first, normed[:, lo : lo + 256]))
            high = over(normed[keys, lo : lo + HD], normed[keys, lo + HD : lo + 256])
            put(buffer, out, 256, mm(second, high))
            if group == 1:
                v = [value_head(h) for h in range(HEADS)]
                put(buffer, out, 384, mm(first, over(beside(v[2], v[4]), beside(v[3], v[5]))))
                put(buffer, out, 640, mm(second, over(v[3], v[5])))
            return carry

        lax.fori_loop(0, blocks, block_body, 0)
        scatter(buffer, (in_1, in_2, in_3)[group], index)

    pack_qk(0, out_1, OUT + 1)
    pack_qk(1, out_2, OUT + 2)
    pack_qk(2, out_3, OUT + 3)

    code_col = to_i32(as_column(code_row_f))
    rank_col = code_col % TILE
    column = iota((tokens, rows), 1)
    unpack_first[...] = ones_where(column == code_col)
    unpack_low[...] = ones_where(column == jnp.where(rank_col < 4, code_col + 12, none))
    unpack_high_a[...] = ones_where(column == jnp.where(rank_col >= 4, code_col - 4, none))
    unpack_high_b[...] = ones_where(column == jnp.where(rank_col >= 4, code_col + 4, none))

    def own_maps(own_axis, message_axis, shape):
        row = iota(shape, own_axis)
        message = iota(shape, message_axis)
        base = (row // SLOT) * TILE
        slot = row % SLOT
        first = ones_where(message == base + slot)
        low = ones_where((message == base + 12 + slot) & (slot < 4))
        high_a = ones_where((message == base + slot - 4) & (slot >= 4))
        high_b = ones_where((message == base + slot + 4) & (slot >= 4))
        labels = ones_where(message == base + 8 + slot - jnp.where(slot < 8, 0, 4))
        return first, low, high_a, high_b, labels

    first, low, high_a, high_b, label_map = own_maps(0, 1, (192, 256))
    second_a = beside(low, high_a)
    second_b = beside(low, high_b)
    first_t, low_t, high_a_t, high_b_t, _ = own_maps(1, 0, (256, 192))
    back_first = beside(first_t, low_t)
    back_second = beside(high_a_t, high_b_t)

    def message(buffer, src, tile):
        return buffer[src, :, tile * HD : (tile + 1) * HD].reshape(256, HD)

    wait_recv(in_0, OUT)

    def unpack_0(block, carry):
        span = pl.ds(pl.multiple_of(block * 192, 64), 192)
        src = pl.ds(block * 16, 16)
        t0 = message(in_0, src, 0)
        t1 = message(in_0, src, 1)
        value_own[0, span, :] = mm(first, t0).astype(BF16)
        value_own[1, span, :] = mm(second_a, over(t0, t1)).astype(BF16)
        found = mm(label_map, t1)
        early = iota((192, 1), 0) % SLOT < 8
        is_zero = jnp.where(early, found[:, 0:1], found[:, 64:65])
        is_one = jnp.where(early, found[:, 1:2], found[:, 65:66])
        spot = iota((192, HD), 1)
        member = jnp.where(
            spot == 0, is_zero, jnp.where(spot == 1, is_one, 1.0 - is_zero - is_one)
        )
        used = spot < 3
        extend_key[span, :] = jnp.where(used, member, 0.0).astype(BF16)
        extend_query[span, :] = jnp.where(used, FAR * (1.0 - member), 0.0).astype(BF16)
        return carry

    lax.fori_loop(0, blocks, unpack_0, 0)
    load_cotangent.wait()

    factor = HD**-0.5
    scale = factor * math.log2(math.e)
    chunk = 256 if own % 256 == 0 else own

    def attention_group(group):
        buffer = (in_1, in_2, in_3)[group]
        wait_recv(buffer, OUT + 1 + group)

        def unpack_body(block, carry):
            span = pl.ds(pl.multiple_of(block * 192, 64), 192)
            src = pl.ds(block * 16, 16)
            t0, t1, t2 = (message(buffer, src, i) for i in range(3))
            q = mm(first, beside(t0, t1)).astype(BF16)
            query_own[0, span, :] = q[:, 0:HD]
            query_own[1, span, :] = q[:, HD : 2 * HD]
            key_own[0, span, :] = mm(second_a, over(t0, t2)).astype(BF16)
            key_own[1, span, :] = mm(second_b, over(t1, t2)).astype(BF16)
            if group == 1:
                t0, t1, t2 = (message(buffer, src, i) for i in range(3, 6))
                v = mm(first, beside(t0, t1)).astype(BF16)
                value_own[2, span, :] = v[:, 0:HD]
                value_own[4, span, :] = v[:, HD : 2 * HD]
                value_own[3, span, :] = mm(second_a, over(t0, t2)).astype(BF16)
                value_own[5, span, :] = mm(second_b, over(t1, t2)).astype(BF16)
            return carry

        lax.fori_loop(0, blocks, unpack_body, 0)
        key_sum[...] = jnp.zeros((2, HD, own), F32)
        value_sum[...] = jnp.zeros((2, HD, own), F32)

        def row_body(index, carry):
            span = pl.ds(pl.multiple_of(index * chunk, chunk), chunk)
            for local in range(2):
                head = 2 * group + local
                cols = slice(head * HD, (head + 1) * HD)
                keys = key_own[local]
                values = value_own[head]
                q = query_own[local, span, :]
                cot = cotangent_ref[span, cols]
                scores = mm_nt(beside(q, extend_query[span, :]), beside(keys, extend_key[...]))
                raised = jnp.exp2((scores - jnp.max(scores, axis=1, keepdims=True)) * scale)
                weights = (raised * (1.0 / jnp.sum(raised, axis=1, keepdims=True))).astype(BF16)
                attended = mm(weights, values).astype(BF16)
                attended_ref[span, cols] = attended
                delta = jnp.sum(cot.astype(F32) * attended.astype(F32), axis=1, keepdims=True)
                grad_weights = mm_nt(cot, values)
                grad_scores = (weights.astype(F32) * (grad_weights - delta)).astype(BF16)
                grad_query_own[local, span, :] = (mm(grad_scores, keys) * factor).astype(BF16)
                value_sum[local] += mm(cot.T, weights)
                key_sum[local] += mm(q.T, grad_scores)
            return carry

        lax.fori_loop(0, own // chunk, row_body, 0)
        for local in range(2):
            grad_key_own[local] = (key_sum[local].T * factor).astype(BF16)
            grad_value_own[2 * group + local] = value_sum[local].T.astype(BF16)

        target = (back_0, back_1, back_2)[group]

        def pack_body(block, carry):
            span = pl.ds(pl.multiple_of(block * 192, 64), 192)
            out = pl.ds(block * 16, 16)
            q = beside(grad_query_own[0, span, :], grad_query_own[1, span, :])
            k = [grad_key_own[i, span, :] for i in range(2)]
            put(target, out, 0, mm(back_first, over(q, beside(k[0], k[1]))))
            put(target, out, 256, mm(back_second, over(k[0], k[1])))
            if group == 1:
                v = [grad_value_own[i, span, :] for i in range(4)]
                put(
                    target, out, 384, mm(back_first, over(beside(v[0], v[2]), beside(v[1], v[3])))
                )
                put(target, out, 640, mm(back_second, over(v[1], v[3])))
            return carry

        lax.fori_loop(0, blocks, pack_body, 0)
        scatter(target, (home_0, home_1, home_2)[group], BACK + group)

    for group in range(3):
        attention_group(group)

    def pack_last(block, carry):
        span = pl.ds(pl.multiple_of(block * 192, 64), 192)
        out = pl.ds(block * 16, 16)
        v4 = grad_value_own[4, span, :]
        v5 = grad_value_own[5, span, :]
        put(back_3, out, 0, mm(back_first, over(v4, v5)))
        put(back_3, out, HD, mm(high_a_t, v5))
        return carry

    lax.fori_loop(0, blocks, pack_last, 0)
    scatter(back_3, home_3, BACK + 3)
    save_attended = pltpu.make_async_copy(attended_ref, attended_hbm, local_sems.at[1])
    save_attended.start()

    near = my_y * size_c + my_c
    near_count = size_y * size_c
    center_query_ref[...] = jnp.zeros((tokens, HD), F32)
    center_key_ref[...] = jnp.zeros((tokens, HD), F32)
    gain_near[near] = jnp.zeros((16, HD), F32)

    def home_group(group):
        buffer = (home_0, home_1, home_2)[group]
        wait_recv(buffer, BACK + group)
        tile = lambda i: buffer[:, :, i * HD : (i + 1) * HD].reshape(rows, HD)
        both = beside(tile(0), tile(1))
        queries = mm(unpack_first[...], both)
        keys = mm(unpack_low[...], both)
        high = (mm(unpack_high_a[...], tile(2)), mm(unpack_high_b[...], tile(2)))
        for local in range(2):
            h = 2 * group + local
            cols = slice(h * HD, (h + 1) * HD)
            part = slice(local * HD, (local + 1) * HD)
            grad_q = queries[:, part].astype(BF16)
            grad_k = (keys[:, part] + high[local]).astype(BF16)
            grad_qn[:, cols] = grad_q
            grad_kn[:, cols] = grad_k
            term = grad_q.astype(F32) * unit_query(h)
            gain_near[near, h : h + 1, :] = jnp.sum(term, axis=0, keepdims=True)
            center_query_ref[...] += gain_of(gain_query_ref, h) * term
            term = grad_k.astype(F32) * unit_key(h)
            gain_near[near, 8 + h : 9 + h, :] = jnp.sum(term, axis=0, keepdims=True)
            center_key_ref[...] += gain_of(gain_key_ref, h) * term

    for group in range(3):
        home_group(group)

    stat_center[my_x] = jnp.where(
        half,
        jnp.sum(center_query_ref[...], axis=1, keepdims=True),
        jnp.sum(center_key_ref[...], axis=1, keepdims=True),
    )
    share(stat_center, my_x, tensors, lambda to: {"tensor": to}, CENTER)
    share(
        gain_near,
        near,
        near_count,
        lambda to: {"dp": ((to // size_c) * size_z + my_z) * size_c + to % size_c},
        NEAR,
    )

    def value_home(buffer, start, h):
        tile = lambda i: buffer[:, :, (start + i) * HD : (start + i + 1) * HD].reshape(rows, HD)
        both = beside(tile(0), tile(1))
        evens = mm(unpack_first[...], both)
        odds = mm(unpack_low[...], both)
        high = (mm(unpack_high_a[...], tile(2)), mm(unpack_high_b[...], tile(2)))
        for i in range(2):
            part = slice(i * HD, (i + 1) * HD)
            at = (h + 2 * i) * HD
            grad_value_ref[:, at : at + HD] = evens[:, part].astype(BF16)
            grad_value_ref[:, at + HD : at + 2 * HD] = (odds[:, part] + high[i]).astype(BF16)

    value_home(home_1, 3, 0)

    share_wait(gain_near, near_count, NEAR)
    total = gain_near[0]
    for i in range(1, near_count):
        total = total + gain_near[i]
    gain_far[my_z] = total
    share(
        gain_far,
        my_z,
        size_z,
        lambda to: {"dp": (my_y * size_z + to) * size_c + my_c},
        FARTHER,
    )

    share_wait(stat_center, tensors, CENTER)
    total = stat_center[0]
    for x in range(1, tensors):
        total = total + stat_center[x]
    total = total / feat_total
    center_q = jnp.broadcast_to(total[:, 0:1], (tokens, HD))
    center_k = jnp.broadcast_to(total[:, 64:65], (tokens, HD))
    for h in range(HEADS):
        cols = slice(h * HD, (h + 1) * HD)
        scaled = gain_of(gain_query_ref, h) * grad_qn[:, cols].astype(F32)
        grad_query_ref[:, cols] = (
            (scaled - unit_query(h) * center_q) * inverse_query_ref[...]
        ).astype(BF16)
        scaled = gain_of(gain_key_ref, h) * grad_kn[:, cols].astype(F32)
        grad_key_ref[:, cols] = (
            (scaled - unit_key(h) * center_k) * inverse_key_ref[...]
        ).astype(BF16)

    share_wait(gain_far, size_z, FARTHER)
    total = gain_far[0]
    for i in range(1, size_z):
        total = total + gain_far[i]
    for h in range(HEADS):
        gain_query_out[h * HD : (h + 1) * HD] = total[h : h + 1].reshape(HD)
        gain_key_out[h * HD : (h + 1) * HD] = total[8 + h : 9 + h].reshape(HD)

    wait_recv(home_3, BACK + 3)
    t0, t1 = (home_3[:, :, i * HD : (i + 1) * HD].reshape(rows, HD) for i in range(2))
    grad_value_ref[:, 4 * HD : 5 * HD] = mm(unpack_first[...], t0).astype(BF16)
    grad_value_ref[:, 5 * HD : 6 * HD] = (
        mm(unpack_low[...], t0) + mm(unpack_high_a[...], t1)
    ).astype(BF16)

    save_attended.wait()
    for i, buffer in enumerate((out_0, out_1, out_2, out_3, back_0, back_1, back_2, back_3)):
        wait_send(buffer, OUT + i, dp - 1)
    wait_send(stat_norm, NORM, tensors - 1)
    wait_send(stat_center, CENTER, tensors - 1)
    wait_send(gain_near, NEAR, near_count - 1)
    wait_send(gain_far, FARTHER, size_z - 1)


def copy_out(*refs):
    count = len(refs) // 2
    sources, targets, sems = refs[:count], refs[count : 2 * count], refs[-1]
    copies = [
        pltpu.make_async_copy(source, target, sems.at[i])
        for i, (source, target) in enumerate(zip(sources, targets))
    ]
    for copy in copies:
        copy.start()
    for copy in copies:
        copy.wait()


def shards(query_raw, key_raw, value_rows, gain_query, gain_key, owner_id, utterance, cotangent):
    dp = lax.axis_size("dp")
    tensors = lax.axis_size("tensor")
    tokens, feat = query_raw.shape
    rows = dp * TILE
    own = dp * SLOT
    _, size_z, _ = SHAPES[dp]
    vmem = pl.BlockSpec(memory_space=pltpu.VMEM)
    anywhere = pl.BlockSpec(memory_space=pl.ANY)
    out_shape = (
        jax.ShapeDtypeStruct((own, feat), BF16),
        jax.ShapeDtypeStruct((tokens, feat), BF16),
        jax.ShapeDtypeStruct((tokens, feat), BF16),
        jax.ShapeDtypeStruct((tokens, feat), BF16),
        jax.ShapeDtypeStruct((feat,), F32),
        jax.ShapeDtypeStruct((feat,), F32),
    )
    first_out = [pltpu.VMEM((dp, TILE, width), BF16) for width in (256, 384, 768, 384)]
    last_back = [pltpu.VMEM((dp, TILE, width), BF16) for width in (384, 768, 384, 256)]
    scratch = (
        [
            pltpu.VMEM((rows, 2 * tokens), BF16),
            pltpu.VMEM((rows, 2 * tokens), BF16),
            pltpu.VMEM((tokens, rows), BF16),
            pltpu.VMEM((tokens, rows), BF16),
            pltpu.VMEM((tokens, rows), BF16),
            pltpu.VMEM((tokens, rows), BF16),
            pltpu.VMEM((2 * tokens, feat), BF16),
            pltpu.VMEM((tokens, HD), F32),
            pltpu.VMEM((tokens, HD), F32),
        ]
        + first_out * 2
        + last_back * 2
        + [
            pltpu.VMEM((HEADS, own, HD), BF16),
            pltpu.VMEM((HEADS, own, HD), BF16),
            pltpu.VMEM((own, HD), BF16),
            pltpu.VMEM((own, HD), BF16),
            pltpu.VMEM((2, own, HD), BF16),
            pltpu.VMEM((2, own, HD), BF16),
            pltpu.VMEM((2, own, HD), BF16),
            pltpu.VMEM((2, own, HD), BF16),
            pltpu.VMEM((2, HD, own), F32),
            pltpu.VMEM((2, HD, own), F32),
            pltpu.VMEM((tokens, feat), BF16),
            pltpu.VMEM((tokens, feat), BF16),
            pltpu.VMEM((tokens, HD), F32),
            pltpu.VMEM((tokens, HD), F32),
            pltpu.VMEM((tensors, tokens, HD), F32),
            pltpu.VMEM((tensors, tokens, HD), F32),
            pltpu.VMEM((dp // size_z, 16, HD), F32),
            pltpu.VMEM((size_z, 16, HD), F32),
            pltpu.VMEM((own, feat), BF16),
            pltpu.VMEM((own, feat), BF16),
            pltpu.SemaphoreType.DMA((12,)),
            pltpu.SemaphoreType.DMA((12,)),
            pltpu.SemaphoreType.DMA((2,)),
        ]
    )
    results = pl.pallas_call(
        functools.partial(kernel, dp, tensors, tokens),
        out_shape=out_shape,
        in_specs=[vmem] * 7 + [anywhere],
        out_specs=[anywhere] + [vmem] * 5,
        scratch_shapes=scratch,
        compiler_params=pltpu.CompilerParams(
            has_side_effects=True, vmem_limit_bytes=58 * 1024 * 1024
        ),
    )(
        query_raw,
        key_raw,
        value_rows,
        gain_query,
        gain_key,
        owner_id,
        utterance,
        cotangent,
    )
    return pl.pallas_call(
        copy_out,
        out_shape=out_shape,
        in_specs=[anywhere] * 6,
        out_specs=[anywhere] * 6,
        scratch_shapes=[pltpu.SemaphoreType.DMA((6,))],
        compiler_params=pltpu.CompilerParams(vmem_limit_bytes=58 * 1024 * 1024),
    )(*results)


def solution(mesh):
    wide = P("dp", "tensor")
    return jax.shard_map(
        shards,
        mesh=mesh,
        in_specs=(wide, wide, wide, P("tensor"), P("tensor"), P("dp"), P("dp"), wide),
        out_specs=(wide, wide, wide, wide, P("tensor"), P("tensor")),
        check_vma=False,
    )
```

time: 202 us -> 281 us (1.39)
  Pallas kernels: 190 us -> 280 us
  local copies, waits for them, and re-layouts: 11.4 us -> 0 us
    pallas_call x0 -> x1, Pallas kernels: none -> 90.7 us  [shards(): pl.pallas_call(copy_out, out_shape=out_shape, in_specs=[anywhere] * 6, ou...]
    broadcast_in_dim x4 -> x0, local copies, waits for them, and re-layouts: 5.02 us -> none  [the longest x1 1.27 us: shards(): gain_query[None, :]]
    unnamed x10 -> x0, local copies, waits for them, and re-layouts: 4.91 us -> none
where the time goes in v1:
time: 281 us; the launch traced here: 280 us
  Pallas kernels  280 us (100%)
    pallas_call x1, Pallas kernels, shards(): pl.pallas_call(functools.partial(kernel, dp, tensors, tokens), out_shape=...  189 us
    pallas_call x1, Pallas kernels, shards(): pl.pallas_call(copy_out, out_shape=out_shape, in_specs=[anywhere] * 6, ou...  90.7 us

profile of v1, /device:TPU:1, one launch (start us, length us, event | category | flops | bytes accessed | tf_op | source)
XLA Modules:
  0.0 280.4 jit_solution(13574279848725734500)
XLA Ops:
  0.6 188.9 %shard_map.127 = (bf16[768,768]{1,0:T(8,128)(2,1)}, bf16[384,768]{1,0:T(8,128)(2,1)}, bf16[384,768]{1,0:T(8,128)(2,1)}, bf16[384,768]{1,0:T(8,128)(2,1)}, f32[768]{0:T(1024)}, /*index=5*/f32[768]{0:T(1024)}) custom-call(bf16[384,768]{1,0:T(8,128)(2,1)} %query_ref.1, bf16[384,768]{1,0:T(8,128)(2,1)} %key_ref.1, bf16[384,768]{1,0:T(8,128)(2,1)} %value_ref.1, ...), custom_call_target="tpu_custom_call" | custom-call | tf_op jit(solution)/shard_map/pallas_call | solution.py:622
  189.6 90.7 %shard_map.128 = (bf16[768,768]{1,0:T(8,128)(2,1)}, bf16[384,768]{1,0:T(8,128)(2,1)}, bf16[384,768]{1,0:T(8,128)(2,1)}, bf16[384,768]{1,0:T(8,128)(2,1)}, f32[768]{0:T(1024)}, /*index=5*/f32[768]{0:T(1024)}) custom-call(bf16[768,768]{1,0:T(8,128)(2,1)} %get-tuple-element.12.refs_0_, bf16[384,768]{1,0:T(8,128)(2,1)} %get-tuple-element.13.refs_1_, ...), custom_call_target="tpu_custom_call" | custom-call | tf_op jit(solution)/shard_map/pallas_call | solution.py:641

commit v2 on v1

--- a/solution.py
+++ b/solution.py
@@ -18,7 +18,7 @@
 F32 = jnp.float32
 BF16 = jnp.bfloat16
 MESH = pl.DeviceIdType.MESH
-STRIDE = 23
+ORDER = {8: (3, -1, 2, -2, 0, -3, 1, 4), 4: (-1, 1, 0, 2)}
 SHAPES = {64: (4, 8, 2), 16: (2, 4, 2)}
 
 
@@ -78,17 +78,25 @@
     inverse_query_ref,
     inverse_key_ref,
     out_0,
+    out_0_lent,
     out_1,
+    out_1_lent,
     out_2,
+    out_2_lent,
     out_3,
+    out_3_lent,
     in_0,
     in_1,
     in_2,
     in_3,
     back_0,
+    back_0_lent,
     back_1,
+    back_1_lent,
     back_2,
+    back_2_lent,
     back_3,
+    back_3_lent,
     home_0,
     home_1,
     home_2,
@@ -107,6 +115,12 @@
     grad_kn,
     center_query_ref,
     center_key_ref,
+    relay_1,
+    relay_2,
+    relay_3,
+    relay_4,
+    relay_5,
+    relay_6,
     stat_norm,
     stat_center,
     gain_near,
@@ -129,22 +143,65 @@
     feat_total = feat * tensors
     blocks = dp // 16
 
-    def scatter(source, target, index):
-        pltpu.make_async_copy(source.at[me], target.at[me], recv_sems.at[index]).start()
+    chips = size_y * size_z
+    my_chip = my_y * size_z + my_z
+    half_way, quarter = size_z // 2, size_z // 4
+    z_of = {
+        step: lax.rem(my_z + step + size_z, size_z) for step in ORDER[size_z] + (-quarter, quarter)
+    }
+    y_of = [lax.rem(my_y + step, size_y) for step in range(size_y)]
+
+    def put_to(source, target, send_index, recv_index, chip, core):
+        pltpu.make_async_remote_copy(
+            src_ref=source,
+            dst_ref=target,
+            send_sem=send_sems.at[send_index],
+            recv_sem=recv_sems.at[recv_index],
+            device_id={"dp": chip * size_c + core},
+            device_id_type=MESH,
+        ).start()
+
+    def lend(outgoing, index):
+        buffer, lent = outgoing
+        put_to(lent, buffer.at[:, my_c], LENT + index, LENT + index, my_chip, 1 - my_c)
+
+    def pair_of(target, chip):
+        return target.at[pl.ds(chip * size_c, size_c)]
+
+    def scatter(outgoing, target, index, relay=None):
+        buffer, lent = outgoing
+        pltpu.make_async_copy(lent, lent, recv_sems.at[LENT + index]).wait()
+        if relay is not None:
+            for step in range(size_y):
+                chip = y_of[step] * size_z + z_of[half_way]
+                over_chip = y_of[step] * size_z + z_of[quarter if step % 2 == 0 else -quarter]
+                put_to(buffer.at[chip], relay.at[step], index, RELAY + index, over_chip, my_c)
+        pltpu.make_async_copy(
+            buffer.at[my_chip], pair_of(target, my_chip), recv_sems.at[index]
+        ).start()
 
         def step_body(step, carry):
-            peer = lax.rem(me + step * STRIDE, dp)
-            pltpu.make_async_remote_copy(
-                src_ref=source.at[peer],
-                dst_ref=target.at[me],
-                send_sem=send_sems.at[index],
-                recv_sem=recv_sems.at[index],
-                device_id={"dp": peer},
-                device_id_type=MESH,
-            ).start()
+            for place, step_z in enumerate(ORDER[size_z]):
+                chip = lax.rem(my_y + step + place, size_y) * size_z + z_of[step_z]
+
+                def direct(chip=chip):
+                    put_to(buffer.at[chip], pair_of(target, my_chip), index, index, chip, my_c)
+
+                if step_z == 0:
+                    pl.when(step > 0)(direct)
+                elif step_z != half_way or relay is None:
+                    direct()
             return carry
 
-        lax.fori_loop(1, dp, step_body, 0)
+        lax.fori_loop(0, size_y, step_body, 0)
+
+    def pass_on(target, index, relay):
+        pltpu.make_async_copy(relay, relay, recv_sems.at[RELAY + index]).wait()
+        for step in range(size_y):
+            ahead = quarter if step % 2 == 0 else -quarter
+            origin = y_of[(size_y - step) % size_y] * size_z + z_of[-ahead]
+            chip = my_y * size_z + z_of[ahead]
+            put_to(relay.at[step], pair_of(target, origin), RELAY + index, index, chip, my_c)
 
     def wait_recv(target, index):
         pltpu.make_async_copy(target, target, recv_sems.at[index]).wait()
@@ -172,10 +229,31 @@
         part = buffer.at[pl.ds(0, count - 1)]
         pltpu.make_async_copy(part, part, recv_sems.at[index]).wait()
 
-    OUT, BACK, NORM, CENTER, NEAR, FARTHER = 0, 4, 8, 9, 10, 11
-
+    OUT, BACK, LENT, RELAY, NORM, CENTER, NEAR, FARTHER = 0, 4, 8, 16, 24, 25, 26, 27
+
+    barrier = pltpu.get_barrier_semaphore()
+
+    def greet(device_id):
+        pl.semaphore_signal(barrier, inc=1, device_id=device_id, device_id_type=MESH)
+
+    def greet_chip(step, carry):
+        greet({"dp": lax.rem(me + step * size_c, dp)})
+        return carry
+
+    for step in range(1, tensors):
+        greet({"tensor": lax.rem(my_x + step, tensors)})
+    for step in range(size_y):
+        greet({"dp": (y_of[step] * size_z + my_z) * size_c + 1 - my_c})
+    lax.fori_loop(1, chips, greet_chip, 0)
     load_cotangent = pltpu.make_async_copy(cotangent_hbm, cotangent_ref, local_sems.at[0])
     load_cotangent.start()
+
+    out_0, out_1, out_2, out_3 = zip(
+        (out_0, out_1, out_2, out_3), (out_0_lent, out_1_lent, out_2_lent, out_3_lent)
+    )
+    back_0, back_1, back_2, back_3 = zip(
+        (back_0, back_1, back_2, back_3), (back_0_lent, back_1_lent, back_2_lent, back_3_lent)
+    )
 
     half = iota((tokens, HD), 1) < 64
     query_f = query_ref[...].astype(F32)
@@ -185,20 +263,22 @@
         jnp.sum(query_f * query_f, axis=1, keepdims=True),
         jnp.sum(key_f * key_f, axis=1, keepdims=True),
     )
-    share(stat_norm, my_x, tensors, lambda to: {"tensor": to}, NORM)
-
     owner_row = owner_ref[...].reshape(1, tokens)
     chosen = jnp.where(iota((dp, tokens), 0) == owner_row, 1.0, 0.0)
     upper = ones_where(iota((tokens, tokens), 0) < iota((tokens, tokens), 1))
     rank_row = jnp.sum(mm(chosen.astype(BF16), upper) * chosen, axis=0, keepdims=True)
     code_row_f = owner_row.astype(F32) * TILE + rank_row
+
+    def sent_place(peer):
+        return lax.rem(peer + my_c, 2) * 8 + lax.div(lax.rem(peer, 16), 2)
+
     diagonal = iota((tokens, tokens), 0) == iota((tokens, tokens), 1)
 
     def as_column(row):
         return jnp.sum(jnp.where(diagonal, row, 0.0), axis=1, keepdims=True)
 
     rank_row = to_i32(rank_row)
-    code_row = to_i32(code_row_f)
+    code_row = lax.div(owner_row, 16) * 256 + sent_place(owner_row) * TILE + rank_row
     none = -1
 
     utterance_col = to_i32(as_column(utterance_ref[...].reshape(1, tokens).astype(F32)))
@@ -209,13 +289,16 @@
     def value_head(h):
         return value_ref[:, h * HD : (h + 1) * HD]
 
-    def put(buffer, out, lo, part):
+    def put(outgoing, block, lo, part):
+        buffer, lent = outgoing
         width = part.shape[1]
-        buffer[out, :, lo : lo + width] = part.astype(BF16).reshape(16, TILE, width)
+        part = part.astype(BF16)
+        out = pl.ds(block * 8, 8)
+        buffer[out, my_c, :, lo : lo + width] = part[0:128].reshape(8, TILE, width)
+        lent[out, :, lo : lo + width] = part[128:256].reshape(8, TILE, width)
 
     def pack_0(block, carry):
         span = pl.ds(pl.multiple_of(block * 256, 256), 256)
-        out = pl.ds(block * 16, 16)
         row = iota((256, tokens), 0) + block * 256
         first = beside(
             ones_where(row == code_row),
@@ -228,13 +311,24 @@
         third = ones_where(row == jnp.where(rank_row < 8, code_row + 8, none))
         pack_first[span, :] = first
         pack_second[span, :] = second
-        put(out_0, out, 0, mm(first, over(value_head(0), value_head(1))))
-        put(out_0, out, HD, mm(second, over(value_head(1), label_high)) + mm(third, label_low))
+        put(out_0, block, 0, mm(first, over(value_head(0), value_head(1))))
+        put(out_0, block, HD, mm(second, over(value_head(1), label_high)) + mm(third, label_low))
         return carry
 
     lax.fori_loop(0, blocks, pack_0, 0)
+    pl.semaphore_wait(barrier, chips - 1 + tensors - 1 + size_y)
+    share(stat_norm, my_x, tensors, lambda to: {"tensor": to}, NORM)
+    lend(out_0, OUT)
+
+    code_col = to_i32(as_column(code_row_f))
+    rank_col = code_col % TILE
+    column = iota((tokens, rows), 1)
+    unpack_first[...] = ones_where(column == code_col)
+    unpack_low[...] = ones_where(column == jnp.where(rank_col < 4, code_col + 12, none))
+    unpack_high_a[...] = ones_where(column == jnp.where(rank_col >= 4, code_col - 4, none))
+    unpack_high_b[...] = ones_where(column == jnp.where(rank_col >= 4, code_col + 4, none))
+
     scatter(out_0, in_0, OUT)
-
     share_wait(stat_norm, tensors, NORM)
     total = stat_norm[0]
     for x in range(1, tensors):
@@ -263,39 +357,35 @@
 
         def block_body(block, carry):
             span = pl.ds(pl.multiple_of(block * 256, 256), 256)
-            out = pl.ds(block * 16, 16)
             first = pack_first[span, :]
             second = pack_second[span, :]
             keys = slice(tokens, 2 * tokens)
-            put(buffer, out, 0, mm(first, normed[:, lo : lo + 256]))
+            put(buffer, block, 0, mm(first, normed[:, lo : lo + 256]))
             high = over(normed[keys, lo : lo + HD], normed[keys, lo + HD : lo + 256])
-            put(buffer, out, 256, mm(second, high))
+            put(buffer, block, 256, mm(second, high))
             if group == 1:
                 v = [value_head(h) for h in range(HEADS)]
-                put(buffer, out, 384, mm(first, over(beside(v[2], v[4]), beside(v[3], v[5]))))
-                put(buffer, out, 640, mm(second, over(v[3], v[5])))
+                put(buffer, block, 384, mm(first, over(beside(v[2], v[4]), beside(v[3], v[5]))))
+                put(buffer, block, 640, mm(second, over(v[3], v[5])))
             return carry
 
         lax.fori_loop(0, blocks, block_body, 0)
-        scatter(buffer, (in_1, in_2, in_3)[group], index)
+        lend(buffer, index)
 
     pack_qk(0, out_1, OUT + 1)
     pack_qk(1, out_2, OUT + 2)
+    scatter(out_1, in_1, OUT + 1, relay_1)
     pack_qk(2, out_3, OUT + 3)
-
-    code_col = to_i32(as_column(code_row_f))
-    rank_col = code_col % TILE
-    column = iota((tokens, rows), 1)
-    unpack_first[...] = ones_where(column == code_col)
-    unpack_low[...] = ones_where(column == jnp.where(rank_col < 4, code_col + 12, none))
-    unpack_high_a[...] = ones_where(column == jnp.where(rank_col >= 4, code_col - 4, none))
-    unpack_high_b[...] = ones_where(column == jnp.where(rank_col >= 4, code_col + 4, none))
-
-    def own_maps(own_axis, message_axis, shape):
+    scatter(out_2, in_2, OUT + 2, relay_2)
+    pass_on(in_1, OUT + 1, relay_1)
+    scatter(out_3, in_3, OUT + 3, relay_3)
+
+    def own_maps(own_axis, message_axis, shape, place_of):
         row = iota(shape, own_axis)
         message = iota(shape, message_axis)
-        base = (row // SLOT) * TILE
-        slot = row % SLOT
+        device = lax.div(row, SLOT)
+        base = place_of(device) * TILE
+        slot = row - device * SLOT
         first = ones_where(message == base + slot)
         low = ones_where((message == base + 12 + slot) & (slot < 4))
         high_a = ones_where((message == base + slot - 4) & (slot >= 4))
@@ -303,10 +393,10 @@
         labels = ones_where(message == base + 8 + slot - jnp.where(slot < 8, 0, 4))
         return first, low, high_a, high_b, labels
 
-    first, low, high_a, high_b, label_map = own_maps(0, 1, (192, 256))
+    first, low, high_a, high_b, label_map = own_maps(0, 1, (192, 256), lambda device: device)
     second_a = beside(low, high_a)
     second_b = beside(low, high_b)
-    first_t, low_t, high_a_t, high_b_t, _ = own_maps(1, 0, (256, 192))
+    first_t, low_t, high_a_t, high_b_t, _ = own_maps(1, 0, (256, 192), sent_place)
     back_first = beside(first_t, low_t)
     back_second = beside(high_a_t, high_b_t)
 
@@ -399,35 +489,39 @@
 
         def pack_body(block, carry):
             span = pl.ds(pl.multiple_of(block * 192, 64), 192)
-            out = pl.ds(block * 16, 16)
             q = beside(grad_query_own[0, span, :], grad_query_own[1, span, :])
             k = [grad_key_own[i, span, :] for i in range(2)]
-            put(target, out, 0, mm(back_first, over(q, beside(k[0], k[1]))))
-            put(target, out, 256, mm(back_second, over(k[0], k[1])))
+            put(target, block, 0, mm(back_first, over(q, beside(k[0], k[1]))))
+            put(target, block, 256, mm(back_second, over(k[0], k[1])))
             if group == 1:
                 v = [grad_value_own[i, span, :] for i in range(4)]
                 put(
-                    target, out, 384, mm(back_first, over(beside(v[0], v[2]), beside(v[1], v[3])))
+                    target, block, 384, mm(back_first, over(beside(v[0], v[2]), beside(v[1], v[3])))
                 )
-                put(target, out, 640, mm(back_second, over(v[1], v[3])))
+                put(target, block, 640, mm(back_second, over(v[1], v[3])))
             return carry
 
         lax.fori_loop(0, blocks, pack_body, 0)
-        scatter(target, (home_0, home_1, home_2)[group], BACK + group)
-
-    for group in range(3):
-        attention_group(group)
+        lend(target, BACK + group)
+        home = (home_0, home_1, home_2)[group]
+        scatter(target, home, BACK + group, (relay_4, relay_5, relay_6)[group])
+
+    attention_group(0)
+    pass_on(in_2, OUT + 2, relay_2)
+    attention_group(1)
+    pass_on(in_3, OUT + 3, relay_3)
+    attention_group(2)
 
     def pack_last(block, carry):
         span = pl.ds(pl.multiple_of(block * 192, 64), 192)
-        out = pl.ds(block * 16, 16)
         v4 = grad_value_own[4, span, :]
         v5 = grad_value_own[5, span, :]
-        put(back_3, out, 0, mm(back_first, over(v4, v5)))
-        put(back_3, out, HD, mm(high_a_t, v5))
+        put(back_3, block, 0, mm(back_first, over(v4, v5)))
+        put(back_3, block, HD, mm(high_a_t, v5))
         return carry
 
     lax.fori_loop(0, blocks, pack_last, 0)
+    lend(back_3, BACK + 3)
     scatter(back_3, home_3, BACK + 3)
     save_attended = pltpu.make_async_copy(attended_ref, attended_hbm, local_sems.at[1])
     save_attended.start()
@@ -461,8 +555,12 @@
             gain_near[near, 8 + h : 9 + h, :] = jnp.sum(term, axis=0, keepdims=True)
             center_key_ref[...] += gain_of(gain_key_ref, h) * term
 
-    for group in range(3):
-        home_group(group)
+    pass_on(home_0, BACK, relay_4)
+    pass_on(home_1, BACK + 1, relay_5)
+    home_group(0)
+    home_group(1)
+    pass_on(home_2, BACK + 2, relay_6)
+    home_group(2)
 
     stat_center[my_x] = jnp.where(
         half,
@@ -539,8 +637,12 @@
     ).astype(BF16)
 
     save_attended.wait()
-    for i, buffer in enumerate((out_0, out_1, out_2, out_3, back_0, back_1, back_2, back_3)):
-        wait_send(buffer, OUT + i, dp - 1)
+    outgoing = (out_0, out_1, out_2, out_3, back_0, back_1, back_2, back_3)
+    for i, (buffer, lent) in enumerate(outgoing):
+        wait_send(buffer, OUT + i, chips - 1)
+        wait_send(lent, LENT + i, chips)
+    for i, buffer in enumerate((relay_1, relay_2, relay_3, relay_4, relay_5, relay_6)):
+        wait_send(buffer, RELAY + 1 + i, size_y)
     wait_send(stat_norm, NORM, tensors - 1)
     wait_send(stat_center, CENTER, tensors - 1)
     wait_send(gain_near, NEAR, near_count - 1)
@@ -548,16 +650,22 @@
 
 
 def copy_out(*refs):
-    count = len(refs) // 2
-    sources, targets, sems = refs[:count], refs[count : 2 * count], refs[-1]
-    copies = [
-        pltpu.make_async_copy(source, target, sems.at[i])
-        for i, (source, target) in enumerate(zip(sources, targets))
+    count = (len(refs) - 2) // 3
+    sources, targets, held = (refs[i * count : (i + 1) * count] for i in range(3))
+    load_sems, save_sems = refs[-2:]
+    loads = [
+        pltpu.make_async_copy(sources[i], held[i], load_sems.at[i]) for i in range(count)
     ]
-    for copy in copies:
-        copy.start()
-    for copy in copies:
-        copy.wait()
+    saves = [
+        pltpu.make_async_copy(held[i], targets[i], save_sems.at[i]) for i in range(count)
+    ]
+    for load in loads:
+        load.start()
+    for load, save in zip(loads, saves):
+        load.wait()
+        save.start()
+    for save in saves:
+        save.wait()
 
 
 def shards(query_raw, key_raw, value_rows, gain_query, gain_key, owner_id, utterance, cotangent):
@@ -566,7 +674,7 @@
     tokens, feat = query_raw.shape
     rows = dp * TILE
     own = dp * SLOT
-    _, size_z, _ = SHAPES[dp]
+    size_y, size_z, _ = SHAPES[dp]
     vmem = pl.BlockSpec(memory_space=pltpu.VMEM)
     anywhere = pl.BlockSpec(memory_space=pl.ANY)
     out_shape = (
@@ -577,8 +685,17 @@
         jax.ShapeDtypeStruct((feat,), F32),
         jax.ShapeDtypeStruct((feat,), F32),
     )
-    first_out = [pltpu.VMEM((dp, TILE, width), BF16) for width in (256, 384, 768, 384)]
-    last_back = [pltpu.VMEM((dp, TILE, width), BF16) for width in (384, 768, 384, 256)]
+    chips = dp // 2
+
+    def outgoing(*widths):
+        shapes = [
+            shape for w in widths for shape in ((chips, 2, TILE, w), (chips, TILE, w))
+        ]
+        return [pltpu.VMEM(shape, BF16) for shape in shapes]
+
+    def incoming(*widths):
+        return [pltpu.VMEM((dp, TILE, width), BF16) for width in widths]
+
     scratch = (
         [
             pltpu.VMEM((rows, 2 * tokens), BF16),
@@ -591,8 +708,10 @@
             pltpu.VMEM((tokens, HD), F32),
             pltpu.VMEM((tokens, HD), F32),
         ]
-        + first_out * 2
-        + last_back * 2
+        + outgoing(256, 384, 768, 384)
+        + incoming(256, 384, 768, 384)
+        + outgoing(384, 768, 384, 256)
+        + incoming(384, 768, 384, 256)
         + [
             pltpu.VMEM((HEADS, own, HD), BF16),
             pltpu.VMEM((HEADS, own, HD), BF16),
@@ -608,14 +727,17 @@
             pltpu.VMEM((tokens, feat), BF16),
             pltpu.VMEM((tokens, HD), F32),
             pltpu.VMEM((tokens, HD), F32),
+        ]
+        + [pltpu.VMEM((size_y, 2, TILE, width), BF16) for width in (384, 768, 384) * 2]
+        + [
             pltpu.VMEM((tensors, tokens, HD), F32),
             pltpu.VMEM((tensors, tokens, HD), F32),
             pltpu.VMEM((dp // size_z, 16, HD), F32),
             pltpu.VMEM((size_z, 16, HD), F32),
             pltpu.VMEM((own, feat), BF16),
             pltpu.VMEM((own, feat), BF16),
-            pltpu.SemaphoreType.DMA((12,)),
-            pltpu.SemaphoreType.DMA((12,)),
+            pltpu.SemaphoreType.DMA((28,)),
+            pltpu.SemaphoreType.DMA((28,)),
             pltpu.SemaphoreType.DMA((2,)),
         ]
     )
@@ -626,7 +748,7 @@
         out_specs=[anywhere] + [vmem] * 5,
         scratch_shapes=scratch,
         compiler_params=pltpu.CompilerParams(
-            has_side_effects=True, vmem_limit_bytes=58 * 1024 * 1024
+            collective_id=0, has_side_effects=True, vmem_limit_bytes=58 * 1024 * 1024
         ),
     )(
         query_raw,
@@ -643,7 +765,8 @@
         out_shape=out_shape,
         in_specs=[anywhere] * 6,
         out_specs=[anywhere] * 6,
-        scratch_shapes=[pltpu.SemaphoreType.DMA((6,))],
+        scratch_shapes=[pltpu.VMEM(out.shape, out.dtype) for out in out_shape]
+        + [pltpu.SemaphoreType.DMA((6,)), pltpu.SemaphoreType.DMA((6,))],
         compiler_params=pltpu.CompilerParams(vmem_limit_bytes=58 * 1024 * 1024),
     )(*results)
 

time: 281 us -> 227 us (0.81)
  Pallas kernels: 280 us -> 226 us
    pallas_call x1, Pallas kernels: 90.7 us -> 2.97 us  [shards(): pl.pallas_call(copy_out, out_shape=out_shape, in_specs=[anywhere] * 6, ou...]
    pallas_call x1, Pallas kernels: 189 us -> 223 us  [shards(): pl.pallas_call(functools.partial(kernel, dp, tensors, tokens), out_shape=...]
where the time goes in v2:
time: 227 us
  Pallas kernels  226 us (100%)
    pallas_call x1, Pallas kernels, shards(): pl.pallas_call(functools.partial(kernel, dp, tensors, tokens), out_shape=...  223 us

profile of v2, /device:TPU:1, one launch (start us, length us, event | category | flops | bytes accessed | tf_op | source)
XLA Modules:
  0.0 226.7 jit_solution(7317673404314414294)
XLA Ops:
  0.6 222.9 %shard_map.127 = (bf16[768,768]{1,0:T(8,128)(2,1)}, bf16[384,768]{1,0:T(8,128)(2,1)}, bf16[384,768]{1,0:T(8,128)(2,1)}, bf16[384,768]{1,0:T(8,128)(2,1)}, f32[768]{0:T(1024)}, /*index=5*/f32[768]{0:T(1024)}) custom-call(bf16[384,768]{1,0:T(8,128)(2,1)} %query_ref.1, bf16[384,768]{1,0:T(8,128)(2,1)} %key_ref.1, bf16[384,768]{1,0:T(8,128)(2,1)} %value_ref.1, ...), custom_call_target="tpu_custom_call" | custom-call | tf_op jit(solution)/shard_map/pallas_call | solution.py:744
  223.5 3.0 %shard_map.128 = (bf16[768,768]{1,0:T(8,128)(2,1)}, bf16[384,768]{1,0:T(8,128)(2,1)}, bf16[384,768]{1,0:T(8,128)(2,1)}, bf16[384,768]{1,0:T(8,128)(2,1)}, f32[768]{0:T(1024)}, /*index=5*/f32[768]{0:T(1024)}) custom-call(bf16[768,768]{1,0:T(8,128)(2,1)} %get-tuple-element.12.refs_0_, bf16[384,768]{1,0:T(8,128)(2,1)} %get-tuple-element.13.refs_1_, ...), custom_call_target="tpu_custom_call" | custom-call | tf_op jit(solution)/shard_map/pallas_call | solution.py:763

commit v3 on v2

--- a/solution.py
+++ b/solution.py
@@ -115,12 +115,6 @@
     grad_kn,
     center_query_ref,
     center_key_ref,
-    relay_1,
-    relay_2,
-    relay_3,
-    relay_4,
-    relay_5,
-    relay_6,
     stat_norm,
     stat_center,
     gain_near,
@@ -145,10 +139,8 @@
 
     chips = size_y * size_z
     my_chip = my_y * size_z + my_z
-    half_way, quarter = size_z // 2, size_z // 4
-    z_of = {
-        step: lax.rem(my_z + step + size_z, size_z) for step in ORDER[size_z] + (-quarter, quarter)
-    }
+    way = 1 - 2 * my_c
+    z_of = {step: lax.rem(my_z + way * step + size_z, size_z) for step in ORDER[size_z]}
     y_of = [lax.rem(my_y + step, size_y) for step in range(size_y)]
 
     def put_to(source, target, send_index, recv_index, chip, core):
@@ -168,40 +160,36 @@
     def pair_of(target, chip):
         return target.at[pl.ds(chip * size_c, size_c)]
 
-    def scatter(outgoing, target, index, relay=None):
+    def settle(outgoing, target, index):
         buffer, lent = outgoing
         pltpu.make_async_copy(lent, lent, recv_sems.at[LENT + index]).wait()
-        if relay is not None:
-            for step in range(size_y):
-                chip = y_of[step] * size_z + z_of[half_way]
-                over_chip = y_of[step] * size_z + z_of[quarter if step % 2 == 0 else -quarter]
-                put_to(buffer.at[chip], relay.at[step], index, RELAY + index, over_chip, my_c)
         pltpu.make_async_copy(
             buffer.at[my_chip], pair_of(target, my_chip), recv_sems.at[index]
         ).start()
 
-        def step_body(step, carry):
-            for place, step_z in enumerate(ORDER[size_z]):
-                chip = lax.rem(my_y + step + place, size_y) * size_z + z_of[step_z]
-
-                def direct(chip=chip):
-                    put_to(buffer.at[chip], pair_of(target, my_chip), index, index, chip, my_c)
-
-                if step_z == 0:
-                    pl.when(step > 0)(direct)
-                elif step_z != half_way or relay is None:
-                    direct()
+    def send_part(outgoing, target, index, step):
+        buffer, _ = outgoing
+        for place, step_z in enumerate(ORDER[size_z]):
+            chip = lax.rem(my_y + step + place, size_y) * size_z + z_of[step_z]
+
+            def send(chip=chip):
+                put_to(buffer.at[chip], pair_of(target, my_chip), index, index, chip, my_c)
+
+            if step_z == 0:
+                pl.when(step > 0)(send)
+            else:
+                send()
+
+    def send_parts(outgoing, target, index, start, stop):
+        def body(step, carry):
+            send_part(outgoing, target, index, step)
             return carry
 
-        lax.fori_loop(0, size_y, step_body, 0)
-
-    def pass_on(target, index, relay):
-        pltpu.make_async_copy(relay, relay, recv_sems.at[RELAY + index]).wait()
-        for step in range(size_y):
-            ahead = quarter if step % 2 == 0 else -quarter
-            origin = y_of[(size_y - step) % size_y] * size_z + z_of[-ahead]
-            chip = my_y * size_z + z_of[ahead]
-            put_to(relay.at[step], pair_of(target, origin), RELAY + index, index, chip, my_c)
+        lax.fori_loop(start, stop, body, 0)
+
+    def scatter(outgoing, target, index):
+        settle(outgoing, target, index)
+        send_parts(outgoing, target, index, 0, size_y)
 
     def wait_recv(target, index):
         pltpu.make_async_copy(target, target, recv_sems.at[index]).wait()
@@ -229,7 +217,7 @@
         part = buffer.at[pl.ds(0, count - 1)]
         pltpu.make_async_copy(part, part, recv_sems.at[index]).wait()
 
-    OUT, BACK, LENT, RELAY, NORM, CENTER, NEAR, FARTHER = 0, 4, 8, 16, 24, 25, 26, 27
+    OUT, BACK, LENT, NORM, CENTER, NEAR, FARTHER = 0, 4, 8, 16, 17, 18, 19
 
     barrier = pltpu.get_barrier_semaphore()
 
@@ -374,11 +362,10 @@
 
     pack_qk(0, out_1, OUT + 1)
     pack_qk(1, out_2, OUT + 2)
-    scatter(out_1, in_1, OUT + 1, relay_1)
+    scatter(out_1, in_1, OUT + 1)
     pack_qk(2, out_3, OUT + 3)
-    scatter(out_2, in_2, OUT + 2, relay_2)
-    pass_on(in_1, OUT + 1, relay_1)
-    scatter(out_3, in_3, OUT + 3, relay_3)
+    settle(out_2, in_2, OUT + 2)
+    send_part(out_2, in_2, OUT + 2, 0)
 
     def own_maps(own_axis, message_axis, shape, place_of):
         row = iota(shape, own_axis)
@@ -432,7 +419,7 @@
     scale = factor * math.log2(math.e)
     chunk = 256 if own % 256 == 0 else own
 
-    def attention_group(group):
+    def attention_group(group, send_in_chunk):
         buffer = (in_1, in_2, in_3)[group]
         wait_recv(buffer, OUT + 1 + group)
 
@@ -459,6 +446,7 @@
         value_sum[...] = jnp.zeros((2, HD, own), F32)
 
         def row_body(index, carry):
+            send_in_chunk(index)
             span = pl.ds(pl.multiple_of(index * chunk, chunk), chunk)
             for local in range(2):
                 head = 2 * group + local
@@ -503,14 +491,33 @@
 
         lax.fori_loop(0, blocks, pack_body, 0)
         lend(target, BACK + group)
-        home = (home_0, home_1, home_2)[group]
-        scatter(target, home, BACK + group, (relay_4, relay_5, relay_6)[group])
-
-    attention_group(0)
-    pass_on(in_2, OUT + 2, relay_2)
-    attention_group(1)
-    pass_on(in_3, OUT + 3, relay_3)
-    attention_group(2)
+
+    def send_later(outgoing, target, index):
+        chunks = own // chunk
+
+        def in_chunk(position):
+            start = 1 + position * (size_y - 1) // chunks
+            stop = 1 + (position + 1) * (size_y - 1) // chunks
+            send_parts(outgoing, target, index, start, stop)
+
+        return in_chunk
+
+    attention_group(0, send_later(out_2, in_2, OUT + 2))
+    settle(out_3, in_3, OUT + 3)
+    send_part(out_3, in_3, OUT + 3, 0)
+    settle(back_0, home_0, BACK)
+    send_part(back_0, home_0, BACK, 0)
+    rest_out = send_later(out_3, in_3, OUT + 3)
+    rest_back = send_later(back_0, home_0, BACK)
+
+    def both_rests(position):
+        rest_out(position)
+        rest_back(position)
+
+    attention_group(1, both_rests)
+    settle(back_1, home_1, BACK + 1)
+    send_part(back_1, home_1, BACK + 1, 0)
+    attention_group(2, send_later(back_1, home_1, BACK + 1))
 
     def pack_last(block, carry):
         span = pl.ds(pl.multiple_of(block * 192, 64), 192)
@@ -522,6 +529,7 @@
 
     lax.fori_loop(0, blocks, pack_last, 0)
     lend(back_3, BACK + 3)
+    scatter(back_2, home_2, BACK + 2)
     scatter(back_3, home_3, BACK + 3)
     save_attended = pltpu.make_async_copy(attended_ref, attended_hbm, local_sems.at[1])
     save_attended.start()
@@ -555,12 +563,8 @@
             gain_near[near, 8 + h : 9 + h, :] = jnp.sum(term, axis=0, keepdims=True)
             center_key_ref[...] += gain_of(gain_key_ref, h) * term
 
-    pass_on(home_0, BACK, relay_4)
-    pass_on(home_1, BACK + 1, relay_5)
-    home_group(0)
-    home_group(1)
-    pass_on(home_2, BACK + 2, relay_6)
-    home_group(2)
+    for group in range(3):
+        home_group(group)
 
     stat_center[my_x] = jnp.where(
         half,
@@ -641,8 +645,6 @@
     for i, (buffer, lent) in enumerate(outgoing):
         wait_send(buffer, OUT + i, chips - 1)
         wait_send(lent, LENT + i, chips)
-    for i, buffer in enumerate((relay_1, relay_2, relay_3, relay_4, relay_5, relay_6)):
-        wait_send(buffer, RELAY + 1 + i, size_y)
     wait_send(stat_norm, NORM, tensors - 1)
     wait_send(stat_center, CENTER, tensors - 1)
     wait_send(gain_near, NEAR, near_count - 1)
@@ -674,7 +676,7 @@
     tokens, feat = query_raw.shape
     rows = dp * TILE
     own = dp * SLOT
-    size_y, size_z, _ = SHAPES[dp]
+    _, size_z, _ = SHAPES[dp]
     vmem = pl.BlockSpec(memory_space=pltpu.VMEM)
     anywhere = pl.BlockSpec(memory_space=pl.ANY)
     out_shape = (
@@ -727,17 +729,14 @@
             pltpu.VMEM((tokens, feat), BF16),
             pltpu.VMEM((tokens, HD), F32),
             pltpu.VMEM((tokens, HD), F32),
-        ]
-        + [pltpu.VMEM((size_y, 2, TILE, width), BF16) for width in (384, 768, 384) * 2]
-        + [
             pltpu.VMEM((tensors, tokens, HD), F32),
             pltpu.VMEM((tensors, tokens, HD), F32),
             pltpu.VMEM((dp // size_z, 16, HD), F32),
             pltpu.VMEM((size_z, 16, HD), F32),
             pltpu.VMEM((own, feat), BF16),
             pltpu.VMEM((own, feat), BF16),
-            pltpu.SemaphoreType.DMA((28,)),
-            pltpu.SemaphoreType.DMA((28,)),
+            pltpu.SemaphoreType.DMA((20,)),
+            pltpu.SemaphoreType.DMA((20,)),
             pltpu.SemaphoreType.DMA((2,)),
         ]
     )

time: 227 us -> 185 us (0.81)
  Pallas kernels: 226 us -> 184 us
    pallas_call x1, Pallas kernels: 223 us -> 181 us  [shards(): pl.pallas_call(functools.partial(kernel, dp, tensors, tokens), out_shape=...]
where the time goes in v3:
time: 185 us
  Pallas kernels  184 us (99%)
    pallas_call x1, Pallas kernels, shards(): pl.pallas_call(functools.partial(kernel, dp, tensors, tokens), out_shape=...  181 us

profile of v3, /device:TPU:1, one launch (start us, length us, event | category | flops | bytes accessed | tf_op | source)
XLA Modules:
  0.0 184.6 jit_solution(2278017723943502441)
XLA Ops:
  0.6 180.8 %shard_map.127 = (bf16[768,768]{1,0:T(8,128)(2,1)}, bf16[384,768]{1,0:T(8,128)(2,1)}, bf16[384,768]{1,0:T(8,128)(2,1)}, bf16[384,768]{1,0:T(8,128)(2,1)}, f32[768]{0:T(1024)}, /*index=5*/f32[768]{0:T(1024)}) custom-call(bf16[384,768]{1,0:T(8,128)(2,1)} %query_ref.1, bf16[384,768]{1,0:T(8,128)(2,1)} %key_ref.1, bf16[384,768]{1,0:T(8,128)(2,1)} %value_ref.1, ...), custom_call_target="tpu_custom_call" | custom-call | tf_op jit(solution)/shard_map/pallas_call | solution.py:743
  181.4 3.0 %shard_map.128 = (bf16[768,768]{1,0:T(8,128)(2,1)}, bf16[384,768]{1,0:T(8,128)(2,1)}, bf16[384,768]{1,0:T(8,128)(2,1)}, bf16[384,768]{1,0:T(8,128)(2,1)}, f32[768]{0:T(1024)}, /*index=5*/f32[768]{0:T(1024)}) custom-call(bf16[768,768]{1,0:T(8,128)(2,1)} %get-tuple-element.12.refs_0_, bf16[384,768]{1,0:T(8,128)(2,1)} %get-tuple-element.13.refs_1_, ...), custom_call_target="tpu_custom_call" | custom-call | tf_op jit(solution)/shard_map/pallas_call | solution.py:762

commit v4 on v3

--- a/solution.py
+++ b/solution.py
@@ -14,6 +14,7 @@
 TILE = 16
 HEADS = 6
 GROUPS = 3
+PART = 32
 FAR = -(2.0**30)
 F32 = jnp.float32
 BF16 = jnp.bfloat16
@@ -63,8 +64,8 @@
     utterance_ref,
     cotangent_hbm,
     attended_hbm,
-    grad_query_ref,
-    grad_key_ref,
+    grad_query_hbm,
+    grad_key_hbm,
     grad_value_ref,
     gain_query_out,
     gain_key_out,
@@ -121,6 +122,8 @@
     gain_far,
     cotangent_ref,
     attended_ref,
+    grad_query_ref,
+    grad_key_ref,
     send_sems,
     recv_sems,
     local_sems,
@@ -243,14 +246,6 @@
         (back_0, back_1, back_2, back_3), (back_0_lent, back_1_lent, back_2_lent, back_3_lent)
     )
 
-    half = iota((tokens, HD), 1) < 64
-    query_f = query_ref[...].astype(F32)
-    key_f = key_ref[...].astype(F32)
-    stat_norm[my_x] = jnp.where(
-        half,
-        jnp.sum(query_f * query_f, axis=1, keepdims=True),
-        jnp.sum(key_f * key_f, axis=1, keepdims=True),
-    )
     owner_row = owner_ref[...].reshape(1, tokens)
     chosen = jnp.where(iota((dp, tokens), 0) == owner_row, 1.0, 0.0)
     upper = ones_where(iota((tokens, tokens), 0) < iota((tokens, tokens), 1))
@@ -305,8 +300,19 @@
 
     lax.fori_loop(0, blocks, pack_0, 0)
     pl.semaphore_wait(barrier, chips - 1 + tensors - 1 + size_y)
+    lend(out_0, OUT)
+
+    half = iota((tokens, HD), 1) < 64
+    query_f = query_ref[...].astype(F32)
+    key_f = key_ref[...].astype(F32)
+    stat_norm[my_x] = jnp.where(
+        half,
+        jnp.sum(query_f * query_f, axis=1, keepdims=True),
+        jnp.sum(key_f * key_f, axis=1, keepdims=True),
+    )
     share(stat_norm, my_x, tensors, lambda to: {"tensor": to}, NORM)
-    lend(out_0, OUT)
+    scatter(out_0, in_0, OUT)
+
 
     code_col = to_i32(as_column(code_row_f))
     rank_col = code_col % TILE
@@ -316,7 +322,6 @@
     unpack_high_a[...] = ones_where(column == jnp.where(rank_col >= 4, code_col - 4, none))
     unpack_high_b[...] = ones_where(column == jnp.where(rank_col >= 4, code_col + 4, none))
 
-    scatter(out_0, in_0, OUT)
     share_wait(stat_norm, tensors, NORM)
     total = stat_norm[0]
     for x in range(1, tensors):
@@ -419,6 +424,10 @@
     scale = factor * math.log2(math.e)
     chunk = 256 if own % 256 == 0 else own
 
+    def softmax(scores):
+        raised = jnp.exp2((scores - jnp.max(scores, axis=1, keepdims=True)) * scale)
+        return (raised * (1.0 / jnp.sum(raised, axis=1, keepdims=True))).astype(BF16)
+
     def attention_group(group, send_in_chunk):
         buffer = (in_1, in_2, in_3)[group]
         wait_recv(buffer, OUT + 1 + group)
@@ -456,13 +465,20 @@
                 q = query_own[local, span, :]
                 cot = cotangent_ref[span, cols]
                 scores = mm_nt(beside(q, extend_query[span, :]), beside(keys, extend_key[...]))
-                raised = jnp.exp2((scores - jnp.max(scores, axis=1, keepdims=True)) * scale)
-                weights = (raised * (1.0 / jnp.sum(raised, axis=1, keepdims=True))).astype(BF16)
+                weights = over(*(softmax(scores[r : r + PART]) for r in range(0, chunk, PART)))
                 attended = mm(weights, values).astype(BF16)
                 attended_ref[span, cols] = attended
                 delta = jnp.sum(cot.astype(F32) * attended.astype(F32), axis=1, keepdims=True)
                 grad_weights = mm_nt(cot, values)
-                grad_scores = (weights.astype(F32) * (grad_weights - delta)).astype(BF16)
+                grad_scores = over(
+                    *(
+                        (
+                            weights[r : r + PART].astype(F32)
+                            * (grad_weights[r : r + PART] - delta[r : r + PART])
+                        ).astype(BF16)
+                        for r in range(0, chunk, PART)
+                    )
+                )
                 grad_query_own[local, span, :] = (mm(grad_scores, keys) * factor).astype(BF16)
                 value_sum[local] += mm(cot.T, weights)
                 key_sum[local] += mm(q.T, grad_scores)
@@ -625,6 +641,11 @@
             (scaled - unit_key(h) * center_k) * inverse_key_ref[...]
         ).astype(BF16)
 
+    save_query = pltpu.make_async_copy(grad_query_ref, grad_query_hbm, local_sems.at[2])
+    save_key = pltpu.make_async_copy(grad_key_ref, grad_key_hbm, local_sems.at[3])
+    save_query.start()
+    save_key.start()
+
     share_wait(gain_far, size_z, FARTHER)
     total = gain_far[0]
     for i in range(1, size_z):
@@ -641,6 +662,8 @@
     ).astype(BF16)
 
     save_attended.wait()
+    save_query.wait()
+    save_key.wait()
     outgoing = (out_0, out_1, out_2, out_3, back_0, back_1, back_2, back_3)
     for i, (buffer, lent) in enumerate(outgoing):
         wait_send(buffer, OUT + i, chips - 1)
@@ -735,16 +758,18 @@
             pltpu.VMEM((size_z, 16, HD), F32),
             pltpu.VMEM((own, feat), BF16),
             pltpu.VMEM((own, feat), BF16),
+            pltpu.VMEM((tokens, feat), BF16),
+            pltpu.VMEM((tokens, feat), BF16),
             pltpu.SemaphoreType.DMA((20,)),
             pltpu.SemaphoreType.DMA((20,)),
-            pltpu.SemaphoreType.DMA((2,)),
+            pltpu.SemaphoreType.DMA((4,)),
         ]
     )
     results = pl.pallas_call(
         functools.partial(kernel, dp, tensors, tokens),
         out_shape=out_shape,
         in_specs=[vmem] * 7 + [anywhere],
-        out_specs=[anywhere] + [vmem] * 5,
+        out_specs=[anywhere] * 3 + [vmem] * 3,
         scratch_shapes=scratch,
         compiler_params=pltpu.CompilerParams(
             collective_id=0, has_side_effects=True, vmem_limit_bytes=58 * 1024 * 1024

time: 185 us -> 186 us (level)
  no operation moved by 1% of the time
where the time goes in v4:
time: 186 us
  Pallas kernels  185 us (99%)
    pallas_call x1, Pallas kernels, shards(): pl.pallas_call(functools.partial(kernel, dp, tensors, tokens), out_shape=...  182 us

profile of v4, /device:TPU:1, one launch (start us, length us, event | category | flops | bytes accessed | tf_op | source)
XLA Modules:
  0.0 185.9 jit_solution(7270434769566702026)
XLA Ops:
  0.6 182.1 %shard_map.127 = (bf16[768,768]{1,0:T(8,128)(2,1)}, bf16[384,768]{1,0:T(8,128)(2,1)}, bf16[384,768]{1,0:T(8,128)(2,1)}, bf16[384,768]{1,0:T(8,128)(2,1)}, f32[768]{0:T(1024)}, /*index=5*/f32[768]{0:T(1024)}) custom-call(bf16[384,768]{1,0:T(8,128)(2,1)} %query_ref.1, bf16[384,768]{1,0:T(8,128)(2,1)} %key_ref.1, bf16[384,768]{1,0:T(8,128)(2,1)} %value_ref.1, ...), custom_call_target="tpu_custom_call" | custom-call | tf_op jit(solution)/shard_map/pallas_call | solution.py:768
  182.7 3.0 %shard_map.128 = (bf16[768,768]{1,0:T(8,128)(2,1)}, bf16[384,768]{1,0:T(8,128)(2,1)}, bf16[384,768]{1,0:T(8,128)(2,1)}, bf16[384,768]{1,0:T(8,128)(2,1)}, f32[768]{0:T(1024)}, /*index=5*/f32[768]{0:T(1024)}) custom-call(bf16[768,768]{1,0:T(8,128)(2,1)} %get-tuple-element.12.refs_0_, bf16[384,768]{1,0:T(8,128)(2,1)} %get-tuple-element.13.refs_1_, ...), custom_call_target="tpu_custom_call" | custom-call | tf_op jit(solution)/shard_map/pallas_call | solution.py:787

commit v5 on v4

--- a/solution.py
+++ b/solution.py
@@ -75,6 +75,7 @@
     unpack_low,
     unpack_high_a,
     unpack_high_b,
+    unpack_high_pair,
     normed,
     inverse_query_ref,
     inverse_key_ref,
@@ -98,6 +99,9 @@
     back_2_lent,
     back_3,
     back_3_lent,
+    back_high,
+    back_high_lent,
+    back_high_got,
     home_0,
     home_1,
     home_2,
@@ -172,11 +176,12 @@
 
     def send_part(outgoing, target, index, step):
         buffer, _ = outgoing
+        landing = target.at[my_chip] if outgoing is back_3 else pair_of(target, my_chip)
         for place, step_z in enumerate(ORDER[size_z]):
             chip = lax.rem(my_y + step + place, size_y) * size_z + z_of[step_z]
 
             def send(chip=chip):
-                put_to(buffer.at[chip], pair_of(target, my_chip), index, index, chip, my_c)
+                put_to(buffer.at[chip], landing, index, index, chip, my_c)
 
             if step_z == 0:
                 pl.when(step > 0)(send)
@@ -220,7 +225,7 @@
         part = buffer.at[pl.ds(0, count - 1)]
         pltpu.make_async_copy(part, part, recv_sems.at[index]).wait()
 
-    OUT, BACK, LENT, NORM, CENTER, NEAR, FARTHER = 0, 4, 8, 16, 17, 18, 19
+    OUT, BACK, LENT, NORM, CENTER, NEAR, FARTHER, HIGH = 0, 4, 8, 16, 17, 18, 19, 20
 
     barrier = pltpu.get_barrier_semaphore()
 
@@ -242,8 +247,9 @@
     out_0, out_1, out_2, out_3 = zip(
         (out_0, out_1, out_2, out_3), (out_0_lent, out_1_lent, out_2_lent, out_3_lent)
     )
-    back_0, back_1, back_2, back_3 = zip(
-        (back_0, back_1, back_2, back_3), (back_0_lent, back_1_lent, back_2_lent, back_3_lent)
+    back_3 = (back_3, back_3_lent)
+    back_0, back_1, back_2 = zip(
+        (back_0, back_1, back_2), (back_0_lent, back_1_lent, back_2_lent)
     )
 
     owner_row = owner_ref[...].reshape(1, tokens)
@@ -321,6 +327,10 @@
     unpack_low[...] = ones_where(column == jnp.where(rank_col < 4, code_col + 12, none))
     unpack_high_a[...] = ones_where(column == jnp.where(rank_col >= 4, code_col - 4, none))
     unpack_high_b[...] = ones_where(column == jnp.where(rank_col >= 4, code_col + 4, none))
+    half_code = lax.div(code_col, 2) - lax.div(rank_col, 2) + rank_col - 4
+    unpack_high_pair[...] = ones_where(
+        iota((tokens, rows // 2), 1) == jnp.where(rank_col >= 4, half_code, none)
+    )
 
     share_wait(stat_norm, tensors, NORM)
     total = stat_norm[0]
@@ -535,18 +545,33 @@
     send_part(back_1, home_1, BACK + 1, 0)
     attention_group(2, send_later(back_1, home_1, BACK + 1))
 
+    high_t = jnp.where(my_c == 0, high_a_t, high_b_t)
+    last, last_lent = back_3
+
     def pack_last(block, carry):
         span = pl.ds(pl.multiple_of(block * 192, 64), 192)
+        out = pl.ds(block * 8, 8)
         v4 = grad_value_own[4, span, :]
         v5 = grad_value_own[5, span, :]
-        put(back_3, block, 0, mm(back_first, over(v4, v5)))
-        put(back_3, block, HD, mm(high_a_t, v5))
+        part = mm(back_first, over(v4, v5)).astype(BF16)
+        last[out, my_c] = part[0:128].reshape(8, TILE, HD)
+        last_lent[out] = part[128:256].reshape(8, TILE, HD)
+        part = mm(high_t, v5).astype(BF16)
+        back_high[out] = part[0:128].reshape(8, TILE, HD)
+        back_high_lent[out] = part[128:256].reshape(8, TILE, HD)
         return carry
 
     lax.fori_loop(0, blocks, pack_last, 0)
     lend(back_3, BACK + 3)
+    put_to(back_high_lent, back_high_got, HIGH, HIGH, my_chip, 1 - my_c)
     scatter(back_2, home_2, BACK + 2)
-    scatter(back_3, home_3, BACK + 3)
+    pltpu.make_async_copy(last_lent, last_lent, recv_sems.at[LENT + BACK + 3]).wait()
+    pltpu.make_async_copy(back_high_got, back_high_got, recv_sems.at[HIGH]).wait()
+    last[:, 2] = back_high[...] + back_high_got[...]
+    pltpu.make_async_copy(
+        last.at[my_chip], home_3.at[my_chip], recv_sems.at[BACK + 3]
+    ).start()
+    send_parts(back_3, home_3, BACK + 3, 0, size_y)
     save_attended = pltpu.make_async_copy(attended_ref, attended_hbm, local_sems.at[1])
     save_attended.start()
 
@@ -655,10 +680,11 @@
         gain_key_out[h * HD : (h + 1) * HD] = total[8 + h : 9 + h].reshape(HD)
 
     wait_recv(home_3, BACK + 3)
-    t0, t1 = (home_3[:, :, i * HD : (i + 1) * HD].reshape(rows, HD) for i in range(2))
+    t0 = home_3[:, 0:2].reshape(rows, HD)
+    t1 = home_3[:, 2].reshape(chips * TILE, HD)
     grad_value_ref[:, 4 * HD : 5 * HD] = mm(unpack_first[...], t0).astype(BF16)
     grad_value_ref[:, 5 * HD : 6 * HD] = (
-        mm(unpack_low[...], t0) + mm(unpack_high_a[...], t1)
+        mm(unpack_low[...], t0) + mm(unpack_high_pair[...], t1)
     ).astype(BF16)
 
     save_attended.wait()
@@ -668,6 +694,7 @@
     for i, (buffer, lent) in enumerate(outgoing):
         wait_send(buffer, OUT + i, chips - 1)
         wait_send(lent, LENT + i, chips)
+    wait_send(back_high_lent, HIGH, chips)
     wait_send(stat_norm, NORM, tensors - 1)
     wait_send(stat_center, CENTER, tensors - 1)
     wait_send(gain_near, NEAR, near_count - 1)
@@ -678,12 +705,21 @@
     count = (len(refs) - 2) // 3
     sources, targets, held = (refs[i * count : (i + 1) * count] for i in range(3))
     load_sems, save_sems = refs[-2:]
-    loads = [
-        pltpu.make_async_copy(sources[i], held[i], load_sems.at[i]) for i in range(count)
-    ]
-    saves = [
-        pltpu.make_async_copy(held[i], targets[i], save_sems.at[i]) for i in range(count)
-    ]
+    loads, saves = [], []
+    for i in range(count):
+        extent = sources[i].shape[0]
+        pieces = max(1, extent // 192) if len(sources[i].shape) == 2 else 1
+        for piece in range(pieces):
+            part = pl.ds(piece * (extent // pieces), extent // pieces)
+            at = len(loads)
+            loads.append(
+                pltpu.make_async_copy(
+                    sources[i].at[part], held[i].at[part], load_sems.at[at]
+                )
+            )
+            saves.append(
+                pltpu.make_async_copy(held[i].at[part], targets[i].at[part], save_sems.at[at])
+            )
     for load in loads:
         load.start()
     for load, save in zip(loads, saves):
@@ -729,14 +765,18 @@
             pltpu.VMEM((tokens, rows), BF16),
             pltpu.VMEM((tokens, rows), BF16),
             pltpu.VMEM((tokens, rows), BF16),
+            pltpu.VMEM((tokens, rows // 2), BF16),
             pltpu.VMEM((2 * tokens, feat), BF16),
             pltpu.VMEM((tokens, HD), F32),
             pltpu.VMEM((tokens, HD), F32),
         ]
         + outgoing(256, 384, 768, 384)
         + incoming(256, 384, 768, 384)
-        + outgoing(384, 768, 384, 256)
-        + incoming(384, 768, 384, 256)
+        + outgoing(384, 768, 384)
+        + [pltpu.VMEM((chips, 3, TILE, HD), BF16)]
+        + [pltpu.VMEM((chips, TILE, HD), BF16) for _ in range(4)]
+        + incoming(384, 768, 384)
+        + [pltpu.VMEM((chips, 3, TILE, HD), BF16)]
         + [
             pltpu.VMEM((HEADS, own, HD), BF16),
             pltpu.VMEM((HEADS, own, HD), BF16),
@@ -760,8 +800,8 @@
             pltpu.VMEM((own, feat), BF16),
             pltpu.VMEM((tokens, feat), BF16),
             pltpu.VMEM((tokens, feat), BF16),
-            pltpu.SemaphoreType.DMA((20,)),
-            pltpu.SemaphoreType.DMA((20,)),
+            pltpu.SemaphoreType.DMA((21,)),
+            pltpu.SemaphoreType.DMA((21,)),
             pltpu.SemaphoreType.DMA((4,)),
         ]
     )
@@ -790,7 +830,7 @@
         in_specs=[anywhere] * 6,
         out_specs=[anywhere] * 6,
         scratch_shapes=[pltpu.VMEM(out.shape, out.dtype) for out in out_shape]
-        + [pltpu.SemaphoreType.DMA((6,)), pltpu.SemaphoreType.DMA((6,))],
+        + [pltpu.SemaphoreType.DMA((16,)), pltpu.SemaphoreType.DMA((16,))],
         compiler_params=pltpu.CompilerParams(vmem_limit_bytes=58 * 1024 * 1024),
     )(*results)
 

time: 186 us -> 185 us (level)
  no operation moved by 1% of the time
where the time goes in v5:
time: 185 us; the launch traced here: 184 us
  Pallas kernels  184 us (99%)
    pallas_call x1, Pallas kernels, shards(): pl.pallas_call(functools.partial(kernel, dp, tensors, tokens), out_shape=...  181 us

profile of v5, /device:TPU:1, one launch (start us, length us, event | category | flops | bytes accessed | tf_op | source)
XLA Modules:
  0.0 184.5 jit_solution(10676804388656810418)
XLA Ops:
  0.6 180.8 %shard_map.127 = (bf16[768,768]{1,0:T(8,128)(2,1)}, bf16[384,768]{1,0:T(8,128)(2,1)}, bf16[384,768]{1,0:T(8,128)(2,1)}, bf16[384,768]{1,0:T(8,128)(2,1)}, f32[768]{0:T(1024)}, /*index=5*/f32[768]{0:T(1024)}) custom-call(bf16[384,768]{1,0:T(8,128)(2,1)} %query_ref.1, bf16[384,768]{1,0:T(8,128)(2,1)} %key_ref.1, bf16[384,768]{1,0:T(8,128)(2,1)} %value_ref.1, ...), custom_call_target="tpu_custom_call" | custom-call | tf_op jit(solution)/shard_map/pallas_call | solution.py:808
  181.5 2.8 %shard_map.128 = (bf16[768,768]{1,0:T(8,128)(2,1)}, bf16[384,768]{1,0:T(8,128)(2,1)}, bf16[384,768]{1,0:T(8,128)(2,1)}, bf16[384,768]{1,0:T(8,128)(2,1)}, f32[768]{0:T(1024)}, /*index=5*/f32[768]{0:T(1024)}) custom-call(bf16[768,768]{1,0:T(8,128)(2,1)} %get-tuple-element.12.refs_0_, bf16[384,768]{1,0:T(8,128)(2,1)} %get-tuple-element.13.refs_1_, ...), custom_call_target="tpu_custom_call" | custom-call | tf_op jit(solution)/shard_map/pallas_call | solution.py:827
